TPU v7x, 512 devices: a whole 4x8x8 slice. The times are simulated.
512 devices in a mesh: seq: 256 (over y, z_hi, x, core), head: 2 (over z_lo).
Axes of the slice: x: 4, y: 8, z: 8 (z_hi: 4, z_lo: 2; z = z_hi * 2 + z_lo), core: 2. Of those that a mesh axis runs over, the one named last changes fastest.
Arguments:
- queries: bfloat16 [32768, 8, 128], P('seq', 'head'), may hold values from -6 to 6
- keys: bfloat16 [32768, 128], P('seq'), may hold values from -6 to 6
- window_start: int32 [32768], P('seq'), may hold values from 0 to 32767, as said below
Outputs:
- gate_target: float32 [32768, 512], P('seq', 'head')
Inputs may be any that keep to these rules, and one draw needn't show every extreme that they name: window_start[q] <= q for every position q.
All inputs are finite; a program needn't handle non-finite values.
Results may differ from a plain program's by a relative error of at most 0.0003.
Values may be sent and summed in bfloat16 or wider, within the bound.
No kernel may reach another device: no remote copies, remote signals or barrier semaphores. Data moves between devices by JAX's collectives and lax.ppermute only.
A program may use at most 64 MiB of HBM per device.

v0:
```python
import math

import jax
import jax.numpy as jnp
from jax import lax
from jax.sharding import PartitionSpec as P

BLOCK = 64


def body(queries, keys, window_start):
    seq_count = lax.axis_size("seq")
    seq_place = lax.axis_index("seq")
    rows = queries.shape[0]
    heads_here = queries.shape[1]
    width = queries.shape[2]
    nblocks = rows * seq_count // BLOCK
    scale = 1.0 / math.sqrt(width)
    positions = seq_place * rows + jnp.arange(rows, dtype=jnp.int32)
    last_query = jnp.max(positions)
    first_start = jnp.min(window_start)
    nquery = queries.shape[0]
    padded = nblocks + 128
    initial = (
        jnp.full((heads_here, nquery, padded), -1e30, jnp.float32),
        jnp.zeros((heads_here, nquery, padded), jnp.float32),
    )
    piece = lax.all_gather(keys, "seq", axis=0, tiled=True)
    count = piece.shape[0]
    segment = math.gcd(count, 512)
    span = segment // BLOCK + 2
    turns = count // segment

    def one_turn(turn, state):
        offset = turn * segment
        key_rows = lax.dynamic_slice_in_dim(piece, offset, segment, 0)

        def compute(state):
            scores = (
                jnp.einsum("qhd,kd->hqk", queries, key_rows, preferred_element_type=jnp.float32)
                * scale
            )
            key_place = offset + jnp.arange(segment, dtype=jnp.int32)
            allowed = (key_place[None, :] <= positions[:, None]) & (
                key_place[None, :] >= window_start[:, None]
            )
            masked = jnp.where(allowed[None], scores, -1e30)
            row_top = jnp.max(masked, axis=-1)
            weights = jnp.where(allowed[None], jnp.exp(scores - row_top[..., None]), 0.0)
            first_block = offset // BLOCK
            local = key_place // BLOCK - first_block
            selector = (local[:, None] == jnp.arange(span, dtype=jnp.int32)[None, :]).astype(
                jnp.float32
            )
            sums = jnp.einsum("hqk,kw->hqw", weights, selector, precision=lax.Precision.HIGHEST)
            old_top = lax.dynamic_slice_in_dim(state[0], first_block, span, 2)
            old_sum = lax.dynamic_slice_in_dim(state[1], first_block, span, 2)
            new_top = jnp.maximum(old_top, row_top[..., None])
            new_sum = old_sum * jnp.exp(old_top - new_top) + sums * jnp.exp(
                row_top[..., None] - new_top
            )
            return (
                lax.dynamic_update_slice_in_dim(state[0], new_top, first_block, 2),
                lax.dynamic_update_slice_in_dim(state[1], new_sum, first_block, 2),
            )

        needed = (offset <= last_query) & (offset + segment - 1 >= first_start)
        return lax.cond(needed, compute, lambda kept: kept, state)

    block_top, block_sum = lax.fori_loop(0, turns, one_turn, initial)
    block_top = block_top[..., :nblocks]
    block_sum = block_sum[..., :nblocks]
    live = block_sum > 0
    overall = jnp.max(jnp.where(live, block_top, -1e30), axis=-1)
    scaled = jnp.where(live, block_sum * jnp.exp(block_top - overall[..., None]), 0.0)
    masses = scaled / jnp.sum(scaled, axis=-1, keepdims=True)
    partial_mass = jnp.sum(masses, axis=0)
    summed = lax.psum_scatter(partial_mass, "head", scatter_dimension=1, tiled=True)
    all_heads = heads_here * lax.axis_size("head")
    visible = (positions // BLOCK - window_start // BLOCK + 1).astype(jnp.float32)
    return summed / all_heads * visible[:, None]


def solution(mesh):
    placed = (P("seq", "head", None), P("seq", None), P("seq"))
    return jax.shard_map(
        body, mesh=mesh, in_specs=placed, out_specs=P("seq", "head"), check_vma=False
    )
```

profile of v0, /device:TPU:1, one launch (start us, length us, event | category | flops | bytes accessed | tf_op | source)
XLA Modules:
  0.0 542.6 jit_solution(2530578464037629346)
XLA Ops:
  6.5 0.0 all-gather.2.cloned.1.call-start
  6.5 0.7 all-gather.2.cloned.1.call-update
  7.3 0.0 reduce-scatter.2.cloned.1.call-start
  7.3 0.7 fusion.43
  8.0 0.9 copy.7
  8.9 1.3 reduce_min.9
  10.2 0.0 copy-start
  10.2 140.3 %all-gather.2.cloned.1.call-done = bf16[32768,128]{1,0:T(8,128)(2,1)} async-done(((bf16[128,128]{1,0:T(8,128)(2,1)}), bf16[32768,128]{1,0:T(8,128)(2,1)}) %all-gather.2.cloned.1.call-update) | async-done | bytes 8388624 | tf_op jit(solution)/shard_map/all_gather | solution.py:28
  150.5 0.1 broadcast_in_dim.50
  150.6 1.2 broadcast_in_dim.51
  151.8 0.0 copy-done
  151.8 82.3 %while.20 = (s32[]{:T(128)}, f32[4,128,640]{1,2,0:T(8,128)S(1)}, f32[4,128,640]{1,2,0:T(8,128)}, s32[]{:T(128)}, s32[]{:T(128)}, /*index=5*/s32[128]{0:T(128)S(1...) while((s32[]{:T(128)}, f32[4,128,640]{1,2,0:T(8,128)S(1)}, ...), condition=%wide.region_6.7_spmd.clone, body=%wide.region_2.6_spmd.clone.sunk | while | flops 100122776 | bytes 2771968 | solution.py:70
  153.0 4.5 conditional.3
  153.1 0.1 compare_and_fusion
  153.2 1.2 select_reduce_fusion
  154.5 1.4 fusion.3
  155.9 0.2 dynamic_update_slice.8
  156.1 1.4 dynamic_update_slice.9
  234.1 2.9 fusion.50
  237.0 0.0 reduce-scatter.2.cloned.1.call-update
  237.0 297.0 %reduce-scatter.2.cloned.1.call-done = f32[128,256]{0,1:T(8,128)} async-done(((f32[128,512]{0,1:T(8,128)}), f32[128,256]{0,1:T(8,128)}) %reduce-scatter.2.cloned.1.call-update) | async-done | bytes 131088 | tf_op jit(solution)/shard_map/reduce_scatter | solution.py:78
  534.0 0.9 broadcast_multiply_fusion
  535.0 0.8 copy.8
  (131 shorter events, 0.8 us)
Async XLA Ops:
  6.5 144.0 %all-gather.2.cloned.1.call-start = ((), (), s32[]{:S(2)}) async-start(), calls=%async_computation.1 | async-start | bytes 8421376 | tf_op jit(solution)/shard_map/all_gather | solution.py:28
  7.3 526.8 %reduce-scatter.2.cloned.1.call-start = ((), (), s32[]{:S(2)}) async-start(), calls=%async_computation.2 | async-start | bytes 393216 | tf_op jit(solution)/shard_map/reduce_scatter | solution.py:78
  10.2 141.6 %copy-start = (s32[128]{0:T(128)S(1)}, s32[128]{0:T(128)}, u32[]{:S(2)}) copy-start(s32[128]{0:T(128)} %param.9) | copy-start | bytes 1540
Sparse Core Ops, SparseCore 0:
  11.9 138.5 all-gather.1
  237.1 296.8 reduce-scatter.1
where the time goes:
time: 553 us; the launch traced here: 543 us
  waiting for transfers between devices  438 us (79%)
  loops' own time  77.7 us (14%)
  between operations  13.4 us (2%)
  other arithmetic  5.94 us (1%)
    reduce_scatter x1, waiting for transfers between devices, body(): lax.psum_scatter(partial_mass, 'head', scatter_dimension=1, tiled=True)  297 us
    all_gather x1, waiting for transfers between devices, body(): piece = lax.all_gather(keys, 'seq', axis=0, tiled=True)  140 us
    another operation x1, loops' own time, body(): block_top, block_sum = lax.fori_loop(0, turns, one_turn, initial)  77 us
  transfers between devices with their start and end apart: 2, of which 2 were waited for; matrix products, arithmetic and copies ran while one was open for 1% of the time, Pallas kernels for 0%

commit v1 on v0

v1 whole, which is shorter than its diff:
```python
import functools
import math

import jax
import jax.numpy as jnp
import numpy as np
from jax import lax
from jax.experimental import pallas as pl
from jax.experimental.pallas import tpu as pltpu
from jax.sharding import Mesh, PartitionSpec as P

BLOCK = 64
CHUNK = 16
LOW = -1e30
SAFE = 60.0
LOG2E = math.log2(math.e)


def shard_of(index, low, core):
    return index // 16 * 64 + low * 32 + index % 16 * 2 + core


def prepare_kernel(*refs, scale, rows):
    *q_refs, lines_ref, starts_ref, most_ref = refs
    mine = lax.axis_index(GROUP)
    depth = lines_ref.shape[0] // 2
    half = lines_ref.shape[1] // len(q_refs)
    most = jnp.float32(0.0)
    for slot, q_ref in enumerate(q_refs):
        source = mine ^ slot
        raw = q_ref[0:depth, :].astype(jnp.float32)
        most = jnp.maximum(most, jnp.max(jnp.sum(raw * raw, axis=0, keepdims=True)))
        scaled = raw * (scale * LOG2E)
        high = scaled.astype(jnp.bfloat16)
        low = (scaled - high.astype(jnp.float32)).astype(jnp.bfloat16)
        at = pl.ds(pl.multiple_of(source * half, half), half)
        lines_ref[0:depth, at] = high
        lines_ref[depth : 2 * depth, at] = low
        digits = q_ref[depth : depth + 16, 0:rows].astype(jnp.float32)
        starts_ref[pl.ds(source, 1), :] = (digits[0:1, :] * 256.0 + digits[1:2, :]).astype(jnp.int32)
    most_ref[...] = jnp.full_like(most_ref, most)


def score_kernel(most_ref, starts_ref, lines_ref, keys_ref, sums_ref, stat_ref, *refs, members, heads, rows, scale, swap):
    mask_ref, tile_ref, part_ref, top_ref = refs
    group = lax.axis_index(PLACE)
    mine = lax.axis_index(GROUP)
    core = lax.axis_index("core")
    side = core ^ swap
    span = CHUNK * BLOCK
    width = heads * rows
    pair = 2 * rows

    largest = jnp.max(jnp.abs(keys_ref[...]), axis=1).astype(jnp.float32)
    longest = jnp.max(jnp.sum(largest * largest, axis=-1))
    safe = jnp.max(most_ref[...]) * longest * (scale * scale) <= SAFE * SAFE
    sums_ref[...] = jnp.zeros_like(sums_ref)

    starts = [starts_ref[2 * member : 2 * member + 1, :] for member in range(members)]
    first_start = jnp.min(functools.reduce(jnp.minimum, starts))
    last_chunk = group // CHUNK
    first_chunk = jnp.minimum(first_start // (rows * 64), last_chunk)

    def chunk_keys(chunk):
        blocks = [keys_ref[column, chunk * 4 + step] for step in range(4) for column in range(4)]
        keys = jnp.concatenate(blocks, axis=0)
        return jnp.concatenate([keys, keys], axis=1)

    line = lax.broadcasted_iota(jnp.int32, (BLOCK, rows), 0)
    places = [
        shard_of(group, member, core) * rows + lax.broadcasted_iota(jnp.int32, (1, rows), 1) for member in range(members)
    ]

    def fill_mask(chunk, inside, outside):
        for block in range(CHUNK):
            base = (shard_of(chunk * CHUNK + block, mine // 2, side) * 2 + mine % 2) * BLOCK
            for member in range(members):
                allowed = (line >= starts[member] - base) & (line <= places[member] - base)
                mask_ref[member, block * BLOCK : (block + 1) * BLOCK, :] = jnp.where(allowed, inside, outside)

    def scores(keys, at):
        return jnp.dot(keys, lines_ref[:, pl.ds(at, pair)], preferred_element_type=jnp.float32)

    def lines_of(chunk):
        return pl.ds(pl.multiple_of(chunk * CHUNK, CHUNK), CHUNK)

    @pl.when(safe)
    def _():
        def one_chunk(chunk, carry):
            keys = chunk_keys(chunk)
            fill_mask(chunk, 1.0, 0.0)
            tile_ref[0] = scores(keys, 0)
            for tile in range(members * width // pair):
                at = tile * pair
                if at + pair < members * width:
                    tile_ref[(tile + 1) % 2] = scores(keys, at + pair)
                for block in range(CHUNK):
                    lines = slice(block * BLOCK, (block + 1) * BLOCK)
                    mask = mask_ref[at // width, lines, :]
                    for column in range(2):
                        x = tile_ref[tile % 2, lines, column * rows : (column + 1) * rows]
                        weights = jnp.exp2(x) * mask
                        part_ref[2 * tile + column, block * 8 : block * 8 + 8, :] = jnp.sum(
                            weights.reshape(BLOCK // 8, 8, rows), axis=0
                        )
                for column in range(2):
                    total = part_ref[2 * tile + column, pl.ds(0, CHUNK, stride=8), :]
                    for line in range(1, 8):
                        total = total + part_ref[2 * tile + column, pl.ds(line, CHUNK, stride=8), :]
                    sums_ref[lines_of(chunk), at + column * rows : at + (column + 1) * rows] = total
            return carry

        lax.fori_loop(first_chunk, last_chunk + 1, one_chunk, 0)

    def each_tile(visit):
        def one_chunk(chunk, carry):
            fill_mask(chunk, 0.0, LOW)

            def one_tile(tile, carry):
                at = pl.multiple_of(tile * pair, pair)
                mask = mask_ref[at // width]
                visit(chunk, pl.ds(at, pair), scores(chunk_keys(chunk), at) + jnp.concatenate([mask, mask], axis=1))
                return carry

            return lax.fori_loop(0, members * width // pair, one_tile, carry)

        lax.fori_loop(first_chunk, last_chunk + 1, one_chunk, 0)

    @pl.when(jnp.logical_not(safe))
    def _():
        def raise_top(chunk, at, x):
            top_ref[:, at] = jnp.maximum(top_ref[:, at], jnp.max(x, axis=0, keepdims=True))

        def add(chunk, at, x):
            weights = jnp.where(x > 0.5 * LOW, jnp.exp2(jnp.minimum(x - top_ref[:, at], 0.0)), 0.0)
            sums_ref[lines_of(chunk), at] = jnp.sum(weights.reshape(CHUNK, BLOCK, pair), axis=1)

        top_ref[...] = jnp.full_like(top_ref, LOW)
        each_tile(raise_top)
        each_tile(add)

    total = jnp.sum(sums_ref[...], axis=0, keepdims=True)
    top = jnp.where(safe, jnp.zeros_like(total), top_ref[...])
    stat_ref[0:1, :] = jnp.where(total > 0.0, top, LOW)
    stat_ref[1:2, :] = total


def mass_kernel(own_ref, other_ref, stat_ref, mass_ref, *, members, heads, rows):
    mine = lax.axis_index(GROUP)
    tops = [stat_ref[:, 0, :], stat_ref[:, 2, :]]
    top = jnp.max(jnp.maximum(*tops), axis=0, keepdims=True)
    total = stat_ref[:, 1, :] * jnp.exp2(tops[0] - top) + stat_ref[:, 3, :] * jnp.exp2(tops[1] - top)
    total = jnp.sum(total, axis=0, keepdims=True)
    for side, sums_ref in enumerate((own_ref, other_ref)):
        share = jnp.exp2(stat_ref[mine, 2 * side : 2 * side + 1, :] - top) / total
        for member in range(members):
            mass = None
            for head in range(heads):
                at = (member * heads + head) * rows
                term = sums_ref[:, at : at + rows] * share[:, at : at + rows]
                mass = term if mass is None else mass + term
            for run in range(mass_ref.shape[1]):
                mass_ref[member, run, side] = mass[run * 16 : run * 16 + 16, :]


def target_kernel(mass_ref, ws_ref, out_ref, lines_ref, *, devices, rows, heads):
    core = lax.axis_index("core")
    first = shard_of(lax.axis_index(PLACE), lax.axis_index("yl"), core) * rows
    place = first + lax.broadcasted_iota(jnp.int32, (1, rows), 1)
    visible = (place // BLOCK - ws_ref[...] // BLOCK + 1).astype(jnp.float32) * (1.0 / heads)
    for source in range(devices):
        for run in range(mass_ref.shape[1]):
            for side in range(2):
                begin = 2 * shard_of(run * 16, source // 2, core ^ side) + source % 2
                lines_ref[pl.ds(begin, 16, stride=4), :] = mass_ref[source, run, side] * visible
    out_ref[...] = lines_ref[...].T


GROUP = ("yl", "head")
PLACE = ("yh", "zh", "x")


def spread(x, axes):
    copies = jnp.broadcast_to(x[None], (lax.axis_size(axes), *x.shape))
    return lax.all_to_all(copies, axes, 0, 0, tiled=True)


def body(queries, keys, window_start):
    blocks = lax.axis_size(PLACE)
    devices = lax.axis_size(GROUP)
    members = devices // 2
    rows, heads_here, width = queries.shape
    heads = 2 * heads_here
    scale = 1.0 / math.sqrt(width)

    lines = jnp.transpose(queries, (2, 1, 0)).reshape(width, heads_here * rows)
    digits = jnp.stack([window_start // 256, window_start % 256]).astype(jnp.bfloat16)
    digits = jnp.pad(digits, ((0, 14), (0, (heads_here - 1) * rows)))
    lines = jnp.concatenate([lines, digits], axis=0)
    def trade(x, step):
        return lax.ppermute(x, GROUP, [(i, i ^ step) for i in range(devices)])

    own = lax.dynamic_slice_in_dim(keys, lax.axis_index("head") * BLOCK, BLOCK, 0)
    column, lines, across, along = lax.optimization_barrier(
        (spread(own, ("yh", "zh")), lines, trade(lines, 3), trade(lines, 2))
    )
    own_keys = spread(column, "x")
    all_queries = [lines, trade(lines, 1), along, across]

    total_rows = members * heads * rows
    vmem = pl.BlockSpec(memory_space=pltpu.VMEM)
    params = pltpu.CompilerParams(vmem_limit_bytes=32 * 1024 * 1024)

    query_lines, starts, most = pl.pallas_call(
        functools.partial(prepare_kernel, scale=scale, rows=rows),
        out_shape=(
            jax.ShapeDtypeStruct((2 * width, total_rows), jnp.bfloat16),
            jax.ShapeDtypeStruct((devices, rows), jnp.int32),
            jax.ShapeDtypeStruct((8, rows), jnp.float32),
        ),
        in_specs=[vmem] * devices,
        out_specs=(vmem, vmem, vmem),
        compiler_params=params,
        cost_estimate=pl.CostEstimate(flops=10 * width * total_rows, bytes_accessed=2 * 1024 * 1024, transcendentals=0),
        name="prepare",
    )(*all_queries)

    own_keys, query_lines = lax.optimization_barrier((own_keys, query_lines))
    other_keys = lax.ppermute(own_keys, "core", [(0, 1), (1, 0)])

    def score(half_keys, swap):
        return pl.pallas_call(
            functools.partial(score_kernel, members=members, heads=heads, rows=rows, scale=scale, swap=swap),
            out_shape=(
                jax.ShapeDtypeStruct((blocks, total_rows), jnp.float32),
                jax.ShapeDtypeStruct((2, total_rows), jnp.float32),
            ),
            in_specs=[vmem] * 4,
            out_specs=(vmem, vmem),
            scratch_shapes=[
                pltpu.VMEM((members, CHUNK * BLOCK, rows), jnp.float32),
                pltpu.VMEM((2, CHUNK * BLOCK, 2 * rows), jnp.float32),
                pltpu.VMEM((total_rows // rows, CHUNK * 8, rows), jnp.float32),
                pltpu.VMEM((1, total_rows), jnp.float32),
            ],
            compiler_params=params,
            cost_estimate=pl.CostEstimate(
                flops=2 * blocks * BLOCK * width * total_rows,
                bytes_accessed=8 * 1024 * 1024,
                transcendentals=blocks * BLOCK * total_rows,
            ),
            name="score",
        )(most, starts, query_lines, half_keys)

    own_sums, own_stat = score(own_keys, 0)
    other_sums, other_stat = score(other_keys, 1)
    stats = spread(jnp.concatenate([own_stat, other_stat], axis=0), GROUP)
    mass = pl.pallas_call(
        functools.partial(mass_kernel, members=members, heads=heads, rows=rows),
        out_shape=jax.ShapeDtypeStruct((members, blocks // 16, 2, 16, rows), jnp.float32),
        in_specs=[vmem] * 3,
        out_specs=vmem,
        compiler_params=params,
        name="mass",
    )(own_sums, other_sums, stats)
    mass = mass.reshape(devices, blocks // 32, 2, 16, rows)
    mass = lax.all_to_all(mass, GROUP, 0, 0, tiled=True)
    return pl.pallas_call(
        functools.partial(target_kernel, devices=devices, rows=rows, heads=heads),
        out_shape=jax.ShapeDtypeStruct((rows, blocks * devices), jnp.float32),
        in_specs=[vmem] * 2,
        out_specs=vmem,
        scratch_shapes=[pltpu.VMEM((blocks * devices, rows), jnp.float32)],
        compiler_params=params,
        name="target",
    )(mass, window_start.reshape(1, rows))


def solution(mesh):
    grid = Mesh(mesh.devices.reshape(-1, 2, 4, 4, 2, 2), ("yh", "yl", "zh", "x", "core", "head"))
    seq = ("yh", "yl", "zh", "x", "core")
    placed = (P(seq, "head", None), P(seq, None), P(seq))
    return jax.shard_map(body, mesh=grid, in_specs=placed, out_specs=P(seq, "head"), check_vma=False)
```

time: 553 us -> 124 us (0.22)
  the two profiles are of different devices: /device:TPU:1 before, /device:TPU:56 now
where the time goes in v1:
time: 124 us; the launch traced here: 123 us
  Pallas kernels  54.6 us (44%)
  starting transfers between devices  31.3 us (25%)
  waiting for transfers between devices  18.5 us (15%)
  blocking collectives  15 us (12%)
  local copies, waits for them, and re-layouts  3.57 us (3%)
    pallas_call x2, Pallas kernels, score(): pl.pallas_call(functools.partial(score_kernel, members=members, heads=hea...  53.3 us
    all_to_all x2, starting transfers between devices, spread(): return lax.all_to_all(copies, axes, 0, 0, tiled=True)  19.9 us
    ppermute x3, waiting for transfers between devices, trade(): return lax.ppermute(x, GROUP, [(i, i ^ step) for i in range(devices)])  11 us
    ppermute x3, starting transfers between devices, trade(): return lax.ppermute(x, GROUP, [(i, i ^ step) for i in range(devices)])  9.5 us
    all_to_all x1, blocking collectives, spread(): return lax.all_to_all(copies, axes, 0, 0, tiled=True)  7.63 us
    all_to_all x2, waiting for transfers between devices, spread(): return lax.all_to_all(copies, axes, 0, 0, tiled=True)  7.55 us
    all_to_all x1, blocking collectives, body(): mass = lax.all_to_all(mass, GROUP, 0, 0, tiled=True)  7.4 us
  transfers between devices with their start and end apart: 6, of which 4 were waited for; matrix products, arithmetic and copies ran while one was open for 0% of the time, Pallas kernels for 22%

profile of v1, /device:TPU:56, one launch (start us, length us, event | category | flops | bytes accessed | tf_op | source)
XLA Modules:
  0.0 123.2 jit_solution(12019737796639714102)
XLA Ops:
  0.0 0.8 copy-done
  0.8 0.8 broadcast_in_dim.6
  1.5 15.6 %all-to-all-start = ((bf16[16,64,128]{2,1,0:T(8,128)(2,1)}), bf16[16,64,128]{2,1,0:T(8,128)(2,1)S(1)}, u32[]{:S(2)}, u32[]{:S(2)}) async-start(bf16[16,64,128]{2,1,0:T(8,128)(2,1)} %broadcast_in_dim.6), calls=%async_computation | async-start | bytes 524288 | tf_op jit(solution)/shard_map/all_to_all | solution.py:185
  17.1 0.1 copy.4
  17.3 0.0 copy-start.1
  17.3 0.6 copy-done.1
  18.0 4.2 %collective-permute-start = (bf16[144,512]{1,0:T(8,128)(2,1)S(1)}, bf16[144,512]{1,0:T(8,128)(2,1)S(1)}, u32[]{:S(2)}, u32[]{:S(2)}) collective-permute-start(bf16[144,512]{1,0:T(8,128)(2,1)S(1)} %pad_maximum_fusion.refs_0_), channel_id=1, source_target_pairs={{0,65},{1,64},{64,1},{65,0},{2,67},{3,66},{66,3},{67,2},{4,69},{5,... | collective-permute-start | bytes 442376 | tf_op jit(solution)/shard_map/ppermute | solution.py:201
  22.2 2.6 %collective-permute-start.1 = (bf16[144,512]{1,0:T(8,128)(2,1)S(1)}, bf16[144,512]{1,0:T(8,128)(2,1)S(1)}, u32[]{:S(2)}, u32[]{:S(2)}) collective-permute-start(bf16[144,512]{1,0:T(8,128)(2,1)S(1)} %pad_maximum_fusion.refs_0_), channel_id=1, source_target_pairs={{0,64},{1,65},{64,0},{65,1},{2,66},{3,67},{66,2},{67,3},{4,68},{5,... | collective-permute-start | bytes 442376 | tf_op jit(solution)/shard_map/ppermute | solution.py:201
  24.8 4.7 %collective-permute-done.refs_3_ = bf16[144,512]{1,0:T(8,128)(2,1)S(1)} collective-permute-done((bf16[144,512]{1,0:T(8,128)(2,1)S(1)}, bf16[144,512]{1,0:T(8,128)(2,1)S(1)}, u32[]{:S(2)}, u32[]{:S(2)}) %collective-permute-start) | collective-permute-done | bytes 147488 | tf_op jit(solution)/shard_map/ppermute | solution.py:201
  29.4 1.9 %collective-permute-done.1.refs_2_ = bf16[144,512]{1,0:T(8,128)(2,1)S(1)} collective-permute-done((bf16[144,512]{1,0:T(8,128)(2,1)S(1)}, bf16[144,512]{1,0:T(8,128)(2,1)S(1)}, u32[]{:S(2)}, u32[]{:S(2)}) %collective-permute-start.1) | collective-permute-done | bytes 147488 | tf_op jit(solution)/shard_map/ppermute | solution.py:201
  31.4 0.0 all-to-all-done
  31.4 1.2 %broadcast_in_dim.7 = bf16[4,16,64,128]{3,2,1,0:T(8,128)(2,1)} broadcast(bf16[16,64,128]{2,1,0:T(8,128)(2,1)S(1)} %all-to-all-done), dimensions={1,2,3} | broadcast | bytes 1310720 | tf_op jit(solution)/shard_map/broadcast_in_dim | solution.py:184
  32.6 4.3 %all-to-all-start.1 = ((bf16[4,16,64,128]{3,2,1,0:T(8,128)(2,1)}), bf16[4,16,64,128]{3,2,1,0:T(8,128)(2,1)S(1)}, u32[]{:S(2)}, u32[]{:S(2)}) async-start(bf16[4,16,64,128]{3,2,1,0:T(8,128)(2,1)} %broadcast_in_dim.7), calls=%async_computation.1 | async-start | bytes 2097152 | tf_op jit(solution)/shard_map/all_to_all | solution.py:185
  36.9 2.8 %collective-permute-start.2 = (bf16[144,512]{1,0:T(8,128)(2,1)S(1)}, bf16[144,512]{1,0:T(8,128)(2,1)S(1)}, u32[]{:S(2)}, u32[]{:S(2)}) collective-permute-start(bf16[144,512]{1,0:T(8,128)(2,1)S(1)} %pad_maximum_fusion.refs_0_), channel_id=1, source_target_pairs={{0,1},{1,0},{64,65},{65,64},{2,3},{3,2},{66,67},{67,66},{4,5},{5,4... | collective-permute-start | bytes 442376 | tf_op jit(solution)/shard_map/ppermute | solution.py:201
  39.6 4.4 %collective-permute-done.2.refs_1_ = bf16[144,512]{1,0:T(8,128)(2,1)S(1)} collective-permute-done((bf16[144,512]{1,0:T(8,128)(2,1)S(1)}, bf16[144,512]{1,0:T(8,128)(2,1)S(1)}, u32[]{:S(2)}, u32[]{:S(2)}) %collective-permute-start.2) | collective-permute-done | bytes 147488 | tf_op jit(solution)/shard_map/ppermute | solution.py:201
  44.0 0.4 prepare.1
  44.4 7.5 %all-to-all-done.1.keys_ref = bf16[4,16,64,128]{3,2,1,0:T(8,128)(2,1)S(1)} async-done(((bf16[4,16,64,128]{3,2,1,0:T(8,128)(2,1)}), bf16[4,16,64,128]{3,2,1,0:T(8,128)(2,1)S(1)}, u32[]{:S(2)}, u32[]{:S(2)}) %all-to-all-start.1) | async-done | bytes 1048608 | tf_op jit(solution)/shard_map/all_to_all | solution.py:185
  51.9 1.9 %collective-permute-start.3 = (bf16[4,16,64,128]{3,2,1,0:T(8,128)(2,1)S(1)}, bf16[4,16,64,128]{3,2,1,0:T(8,128)(2,1)S(1)}, u32[]{:S(2)}, u32[]{:S(2)}) collective-permute-start(bf16[4,16,64,128]{3,2,1,0:T(8,128)(2,1)S(1)} %all-to-all-done.1.keys_ref), channel_id=1, source_target_pairs={{0,2},{2,0},{1,3},{3,1},{4,6},{6,4},{5,7},{7,5},{8,10},{10,8},{9,1... | collective-permute-start | bytes 3145736 | tf_op jit(solution)/shard_map/ppermute | solution.py:229
  53.8 26.7 %score.2 = (f32[64,2048]{1,0:T(8,128)S(1)}, f32[2,2048]{1,0:T(2,128)S(1)}) custom-call(f32[8,128]{1,0:T(8,128)S(1)} %get-tuple-element.21.most_ref, s32[4,128]{1,0:T(4,128)S(1)} %get-tuple-element.22.starts_ref, bf16[256,2048]{1,0:T(8,128)(2,1)S(1)} %get-tuple-element.25.lines_ref, bf16[4,16,64,128]{3,2,1,0:T(8,128)(2,1)S(1)} %all-to-all-done.1.keys_ref), custom_call_target="tpu_custom_call" | custom-call | flops 2147483648 | bytes 8388608 | tf_op jit(solution)/shard_map/score/pallas_call | solution.py:232
  80.5 26.7 %score.3 = (f32[64,2048]{1,0:T(8,128)S(1)}, f32[2,2048]{1,0:T(2,128)S(1)}) custom-call(f32[8,128]{1,0:T(8,128)S(1)} %get-tuple-element.21.most_ref, s32[4,128]{1,0:T(4,128)S(1)} %get-tuple-element.22.starts_ref, bf16[256,2048]{1,0:T(8,128)(2,1)S(1)} %get-tuple-element.25.lines_ref, bf16[4,16,64,128]{3,2,1,0:T(8,128)(2,1)S(1)} %collective-permute-done.3.keys_ref), custom_call_target="tpu_custom_call" | custom-call | flops 2147483648 | bytes 8388608 | tf_op jit(solution)/shard_map/score/pallas_call | solution.py:232
  107.3 7.6 %all_to_all.20.stat_ref = f32[4,4,2048]{2,1,0:T(4,128)S(1)} all-to-all(f32[4,4,2048]{2,1,0:T(4,128)S(1)} %broadcast_in_dim.8), channel_id=1, replica_groups=mesh['yh'=4,'yl'=2,'zh'=4,'x'=4,'core'=2,'head'=2] {'yl','head'}, dimensions={0} | all-to-all | bytes 262144 | tf_op jit(solution)/shard_map/all_to_all | solution.py:185
  114.9 0.1 mass.1
  115.0 7.4 %all_to_all.21.mass_ref = f32[4,2,2,16,128]{4,3,2,1,0:T(8,128)S(1)} all-to-all(f32[4,2,2,16,128]{4,3,2,1,0:T(8,128)S(1)} %bitcast.11), channel_id=1, replica_groups=mesh['yh'=4,'yl'=2,'zh'=4,'x'=4,'core'=2,'head'=2] {'yl','head'}, dimensions={0} | all-to-all | bytes 262144 | tf_op jit(solution)/shard_map/all_to_all | solution.py:267
  122.4 0.8 target.1
  (11 shorter events, 0.1 us)
Async XLA Ops:
  0.0 0.8 copy-start
  1.5 15.6 %copy-start.2 = (bf16[128,4,128]{2,1,0:T(4,128)(2,1)S(1)}, bf16[128,4,128]{2,1,0:T(4,128)(2,1)}, u32[]{:S(2)}) copy-start(bf16[128,4,128]{2,1,0:T(4,128)(2,1)} %param.3) | copy-start | bytes 393220
  1.5 29.8 %all-to-all-start = ((bf16[16,64,128]{2,1,0:T(8,128)(2,1)}), bf16[16,64,128]{2,1,0:T(8,128)(2,1)S(1)}, u32[]{:S(2)}, u32[]{:S(2)}) async-start(bf16[16,64,128]{2,1,0:T(8,128)(2,1)} %broadcast_in_dim.6), calls=%async_computation | async-start | bytes 524288 | tf_op jit(solution)/shard_map/all_to_all | solution.py:185
  17.3 0.7 copy-start.1
  18.0 11.4 %collective-permute-start = (bf16[144,512]{1,0:T(8,128)(2,1)S(1)}, bf16[144,512]{1,0:T(8,128)(2,1)S(1)}, u32[]{:S(2)}, u32[]{:S(2)}) collective-permute-start(bf16[144,512]{1,0:T(8,128)(2,1)S(1)} %pad_maximum_fusion.refs_0_), channel_id=1, source_target_pairs={{0,65},{1,64},{64,1},{65,0},{2,67},{3,66},{66,3},{67,2},{4,69},{5,... | collective-permute-start | bytes 442376 | tf_op jit(solution)/shard_map/ppermute | solution.py:201
  22.2 9.2 %collective-permute-start.1 = (bf16[144,512]{1,0:T(8,128)(2,1)S(1)}, bf16[144,512]{1,0:T(8,128)(2,1)S(1)}, u32[]{:S(2)}, u32[]{:S(2)}) collective-permute-start(bf16[144,512]{1,0:T(8,128)(2,1)S(1)} %pad_maximum_fusion.refs_0_), channel_id=1, source_target_pairs={{0,64},{1,65},{64,0},{65,1},{2,66},{3,67},{66,2},{67,3},{4,68},{5,... | collective-permute-start | bytes 442376 | tf_op jit(solution)/shard_map/ppermute | solution.py:201
  32.6 19.3 %all-to-all-start.1 = ((bf16[4,16,64,128]{3,2,1,0:T(8,128)(2,1)}), bf16[4,16,64,128]{3,2,1,0:T(8,128)(2,1)S(1)}, u32[]{:S(2)}, u32[]{:S(2)}) async-start(bf16[4,16,64,128]{3,2,1,0:T(8,128)(2,1)} %broadcast_in_dim.7), calls=%async_computation.1 | async-start | bytes 2097152 | tf_op jit(solution)/shard_map/all_to_all | solution.py:185
  36.9 7.1 %collective-permute-start.2 = (bf16[144,512]{1,0:T(8,128)(2,1)S(1)}, bf16[144,512]{1,0:T(8,128)(2,1)S(1)}, u32[]{:S(2)}, u32[]{:S(2)}) collective-permute-start(bf16[144,512]{1,0:T(8,128)(2,1)S(1)} %pad_maximum_fusion.refs_0_), channel_id=1, source_target_pairs={{0,1},{1,0},{64,65},{65,64},{2,3},{3,2},{66,67},{67,66},{4,5},{5,4... | collective-permute-start | bytes 442376 | tf_op jit(solution)/shard_map/ppermute | solution.py:201
  51.9 28.6 %collective-permute-start.3 = (bf16[4,16,64,128]{3,2,1,0:T(8,128)(2,1)S(1)}, bf16[4,16,64,128]{3,2,1,0:T(8,128)(2,1)S(1)}, u32[]{:S(2)}, u32[]{:S(2)}) collective-permute-start(bf16[4,16,64,128]{3,2,1,0:T(8,128)(2,1)S(1)} %all-to-all-done.1.keys_ref), channel_id=1, source_target_pairs={{0,2},{2,0},{1,3},{3,1},{4,6},{6,4},{5,7},{7,5},{8,10},{10,8},{9,1... | collective-permute-start | bytes 3145736 | tf_op jit(solution)/shard_map/ppermute | solution.py:229

commit v2 on v1

--- a/solution.py
+++ b/solution.py
@@ -197,15 +197,15 @@
     digits = jnp.stack([window_start // 256, window_start % 256]).astype(jnp.bfloat16)
     digits = jnp.pad(digits, ((0, 14), (0, (heads_here - 1) * rows)))
     lines = jnp.concatenate([lines, digits], axis=0)
+
     def trade(x, step):
         return lax.ppermute(x, GROUP, [(i, i ^ step) for i in range(devices)])
 
     own = lax.dynamic_slice_in_dim(keys, lax.axis_index("head") * BLOCK, BLOCK, 0)
-    column, lines, across, along = lax.optimization_barrier(
-        (spread(own, ("yh", "zh")), lines, trade(lines, 3), trade(lines, 2))
-    )
+    column, lines, near = lax.optimization_barrier((spread(own, ("yh", "zh")), lines, trade(lines, 1)))
     own_keys = spread(column, "x")
-    all_queries = [lines, trade(lines, 1), along, across]
+    across, along = trade(lines, 3), trade(lines, 2)
+    all_queries = [lines, near, along, across]
 
     total_rows = members * heads * rows
     vmem = pl.BlockSpec(memory_space=pltpu.VMEM)

time: 124 us -> 121 us (0.976)
  waiting for transfers between devices: 18.5 us -> 15.1 us
    all_to_all x2, waiting for transfers between devices: 7.55 us -> 2.46 us  [spread(): return lax.all_to_all(copies, axes, 0, 0, tiled=True)]
    ppermute x3, waiting for transfers between devices: 11 us -> 12.6 us  [trade(): return lax.ppermute(x, GROUP, [(i, i ^ step) for i in range(devices)])]
  transfers between devices with their start and end apart: 6 -> 6, of which waited for: 4 -> 5; matrix products, arithmetic and copies ran while one was open for 0% -> 0% of each run, Pallas kernels for 22% -> 22%
where the time goes in v2:
time: 121 us
  Pallas kernels  54.6 us (45%)
  starting transfers between devices  32.1 us (27%)
  blocking collectives  15.4 us (13%)
  waiting for transfers between devices  15.1 us (12%)
  local copies, waits for them, and re-layouts  3.57 us (3%)
    pallas_call x2, Pallas kernels, score(): pl.pallas_call(functools.partial(score_kernel, members=members, heads=hea...  53.3 us
    all_to_all x2, starting transfers between devices, spread(): return lax.all_to_all(copies, axes, 0, 0, tiled=True)  19.9 us
    ppermute x3, waiting for transfers between devices, trade(): return lax.ppermute(x, GROUP, [(i, i ^ step) for i in range(devices)])  12.6 us
    ppermute x3, starting transfers between devices, trade(): return lax.ppermute(x, GROUP, [(i, i ^ step) for i in range(devices)])  10.3 us
    all_to_all x1, blocking collectives, spread(): return lax.all_to_all(copies, axes, 0, 0, tiled=True)  7.96 us
    all_to_all x1, blocking collectives, body(): mass = lax.all_to_all(mass, GROUP, 0, 0, tiled=True)  7.41 us
    all_to_all x2, waiting for transfers between devices, spread(): return lax.all_to_all(copies, axes, 0, 0, tiled=True)  2.46 us
  transfers between devices with their start and end apart: 6, of which 5 were waited for; matrix products, arithmetic and copies ran while one was open for 0% of the time, Pallas kernels for 22%

profile of v2, /device:TPU:56, one launch (start us, length us, event | category | flops | bytes accessed | tf_op | source)
XLA Modules:
  0.0 120.9 jit_solution(13819294115100960507)
XLA Ops:
  0.0 0.8 copy-done
  0.8 0.8 broadcast_in_dim.6
  1.5 15.6 %all-to-all-start = ((bf16[16,64,128]{2,1,0:T(8,128)(2,1)}), bf16[16,64,128]{2,1,0:T(8,128)(2,1)S(1)}, u32[]{:S(2)}, u32[]{:S(2)}) async-start(bf16[16,64,128]{2,1,0:T(8,128)(2,1)} %broadcast_in_dim.6), calls=%async_computation | async-start | bytes 524288 | tf_op jit(solution)/shard_map/all_to_all | solution.py:185
  17.1 0.1 copy.4
  17.3 0.0 copy-start.1
  17.3 0.6 copy-done.1
  18.0 3.4 %collective-permute-start = (bf16[144,512]{1,0:T(8,128)(2,1)S(1)}, bf16[144,512]{1,0:T(8,128)(2,1)S(1)}, u32[]{:S(2)}, u32[]{:S(2)}) collective-permute-start(bf16[144,512]{1,0:T(8,128)(2,1)S(1)} %pad_maximum_fusion.refs_0_), channel_id=1, source_target_pairs={{0,1},{1,0},{64,65},{65,64},{2,3},{3,2},{66,67},{67,66},{4,5},{5,4... | collective-permute-start | bytes 442376 | tf_op jit(solution)/shard_map/ppermute | solution.py:202
  21.4 7.0 %collective-permute-done.refs_1_ = bf16[144,512]{1,0:T(8,128)(2,1)S(1)} collective-permute-done((bf16[144,512]{1,0:T(8,128)(2,1)S(1)}, bf16[144,512]{1,0:T(8,128)(2,1)S(1)}, u32[]{:S(2)}, u32[]{:S(2)}) %collective-permute-start) | collective-permute-done | bytes 147488 | tf_op jit(solution)/shard_map/ppermute | solution.py:202
  28.4 0.4 all-to-all-done
  28.7 1.2 %broadcast_in_dim.7 = bf16[4,16,64,128]{3,2,1,0:T(8,128)(2,1)} broadcast(bf16[16,64,128]{2,1,0:T(8,128)(2,1)S(1)} %all-to-all-done), dimensions={1,2,3} | broadcast | bytes 1310720 | tf_op jit(solution)/shard_map/broadcast_in_dim | solution.py:184
  30.0 4.3 %all-to-all-start.1 = ((bf16[4,16,64,128]{3,2,1,0:T(8,128)(2,1)}), bf16[4,16,64,128]{3,2,1,0:T(8,128)(2,1)S(1)}, u32[]{:S(2)}, u32[]{:S(2)}) async-start(bf16[4,16,64,128]{3,2,1,0:T(8,128)(2,1)} %broadcast_in_dim.7), calls=%async_computation.1 | async-start | bytes 2097152 | tf_op jit(solution)/shard_map/all_to_all | solution.py:185
  34.3 4.6 %collective-permute-start.1 = (bf16[144,512]{1,0:T(8,128)(2,1)S(1)}, bf16[144,512]{1,0:T(8,128)(2,1)S(1)}, u32[]{:S(2)}, u32[]{:S(2)}) collective-permute-start(bf16[144,512]{1,0:T(8,128)(2,1)S(1)} %pad_maximum_fusion.refs_0_), channel_id=1, source_target_pairs={{0,64},{1,65},{64,0},{65,1},{2,66},{3,67},{66,2},{67,3},{4,68},{5,... | collective-permute-start | bytes 442376 | tf_op jit(solution)/shard_map/ppermute | solution.py:202
  38.9 2.3 %collective-permute-start.2 = (bf16[144,512]{1,0:T(8,128)(2,1)S(1)}, bf16[144,512]{1,0:T(8,128)(2,1)S(1)}, u32[]{:S(2)}, u32[]{:S(2)}) collective-permute-start(bf16[144,512]{1,0:T(8,128)(2,1)S(1)} %pad_maximum_fusion.refs_0_), channel_id=1, source_target_pairs={{0,65},{1,64},{64,1},{65,0},{2,67},{3,66},{66,3},{67,2},{4,69},{5,... | collective-permute-start | bytes 442376 | tf_op jit(solution)/shard_map/ppermute | solution.py:202
  41.2 1.6 %collective-permute-done.1.refs_2_ = bf16[144,512]{1,0:T(8,128)(2,1)S(1)} collective-permute-done((bf16[144,512]{1,0:T(8,128)(2,1)S(1)}, bf16[144,512]{1,0:T(8,128)(2,1)S(1)}, u32[]{:S(2)}, u32[]{:S(2)}) %collective-permute-start.1) | collective-permute-done | bytes 147488 | tf_op jit(solution)/shard_map/ppermute | solution.py:202
  42.8 4.0 %collective-permute-done.2.refs_3_ = bf16[144,512]{1,0:T(8,128)(2,1)S(1)} collective-permute-done((bf16[144,512]{1,0:T(8,128)(2,1)S(1)}, bf16[144,512]{1,0:T(8,128)(2,1)S(1)}, u32[]{:S(2)}, u32[]{:S(2)}) %collective-permute-start.2) | collective-permute-done | bytes 147488 | tf_op jit(solution)/shard_map/ppermute | solution.py:202
  46.8 0.4 prepare.1
  47.2 2.1 %all-to-all-done.1.keys_ref = bf16[4,16,64,128]{3,2,1,0:T(8,128)(2,1)S(1)} async-done(((bf16[4,16,64,128]{3,2,1,0:T(8,128)(2,1)}), bf16[4,16,64,128]{3,2,1,0:T(8,128)(2,1)S(1)}, u32[]{:S(2)}, u32[]{:S(2)}) %all-to-all-start.1) | async-done | bytes 1048608 | tf_op jit(solution)/shard_map/all_to_all | solution.py:185
  49.3 1.9 %collective-permute-start.3 = (bf16[4,16,64,128]{3,2,1,0:T(8,128)(2,1)S(1)}, bf16[4,16,64,128]{3,2,1,0:T(8,128)(2,1)S(1)}, u32[]{:S(2)}, u32[]{:S(2)}) collective-permute-start(bf16[4,16,64,128]{3,2,1,0:T(8,128)(2,1)S(1)} %all-to-all-done.1.keys_ref), channel_id=1, source_target_pairs={{0,2},{2,0},{1,3},{3,1},{4,6},{6,4},{5,7},{7,5},{8,10},{10,8},{9,1... | collective-permute-start | bytes 3145736 | tf_op jit(solution)/shard_map/ppermute | solution.py:229
  51.2 26.7 %score.2 = (f32[64,2048]{1,0:T(8,128)S(1)}, f32[2,2048]{1,0:T(2,128)S(1)}) custom-call(f32[8,128]{1,0:T(8,128)S(1)} %get-tuple-element.19.most_ref, s32[4,128]{1,0:T(4,128)S(1)} %get-tuple-element.20.starts_ref, bf16[256,2048]{1,0:T(8,128)(2,1)S(1)} %get-tuple-element.23.lines_ref, bf16[4,16,64,128]{3,2,1,0:T(8,128)(2,1)S(1)} %all-to-all-done.1.keys_ref), custom_call_target="tpu_custom_call" | custom-call | flops 2147483648 | bytes 8388608 | tf_op jit(solution)/shard_map/score/pallas_call | solution.py:232
  77.9 26.7 %score.3 = (f32[64,2048]{1,0:T(8,128)S(1)}, f32[2,2048]{1,0:T(2,128)S(1)}) custom-call(f32[8,128]{1,0:T(8,128)S(1)} %get-tuple-element.19.most_ref, s32[4,128]{1,0:T(4,128)S(1)} %get-tuple-element.20.starts_ref, bf16[256,2048]{1,0:T(8,128)(2,1)S(1)} %get-tuple-element.23.lines_ref, bf16[4,16,64,128]{3,2,1,0:T(8,128)(2,1)S(1)} %collective-permute-done.3.keys_ref), custom_call_target="tpu_custom_call" | custom-call | flops 2147483648 | bytes 8388608 | tf_op jit(solution)/shard_map/score/pallas_call | solution.py:232
  104.6 8.0 %all_to_all.20.stat_ref = f32[4,4,2048]{2,1,0:T(4,128)S(1)} all-to-all(f32[4,4,2048]{2,1,0:T(4,128)S(1)} %broadcast_in_dim.8), channel_id=1, replica_groups=mesh['yh'=4,'yl'=2,'zh'=4,'x'=4,'core'=2,'head'=2] {'yl','head'}, dimensions={0} | all-to-all | bytes 262144 | tf_op jit(solution)/shard_map/all_to_all | solution.py:185
  112.6 0.1 mass.1
  112.7 7.4 %all_to_all.21.mass_ref = f32[4,2,2,16,128]{4,3,2,1,0:T(8,128)S(1)} all-to-all(f32[4,2,2,16,128]{4,3,2,1,0:T(8,128)S(1)} %bitcast.11), channel_id=1, replica_groups=mesh['yh'=4,'yl'=2,'zh'=4,'x'=4,'core'=2,'head'=2] {'yl','head'}, dimensions={0} | all-to-all | bytes 262144 | tf_op jit(solution)/shard_map/all_to_all | solution.py:267
  120.1 0.8 target.1
  (11 shorter events, 0.1 us)
Async XLA Ops:
  0.0 0.8 copy-start
  1.5 15.6 %copy-start.2 = (bf16[128,4,128]{2,1,0:T(4,128)(2,1)S(1)}, bf16[128,4,128]{2,1,0:T(4,128)(2,1)}, u32[]{:S(2)}) copy-start(bf16[128,4,128]{2,1,0:T(4,128)(2,1)} %param.3) | copy-start | bytes 393220
  1.5 27.2 %all-to-all-start = ((bf16[16,64,128]{2,1,0:T(8,128)(2,1)}), bf16[16,64,128]{2,1,0:T(8,128)(2,1)S(1)}, u32[]{:S(2)}, u32[]{:S(2)}) async-start(bf16[16,64,128]{2,1,0:T(8,128)(2,1)} %broadcast_in_dim.6), calls=%async_computation | async-start | bytes 524288 | tf_op jit(solution)/shard_map/all_to_all | solution.py:185
  17.3 0.7 copy-start.1
  18.0 10.4 %collective-permute-start = (bf16[144,512]{1,0:T(8,128)(2,1)S(1)}, bf16[144,512]{1,0:T(8,128)(2,1)S(1)}, u32[]{:S(2)}, u32[]{:S(2)}) collective-permute-start(bf16[144,512]{1,0:T(8,128)(2,1)S(1)} %pad_maximum_fusion.refs_0_), channel_id=1, source_target_pairs={{0,1},{1,0},{64,65},{65,64},{2,3},{3,2},{66,67},{67,66},{4,5},{5,4... | collective-permute-start | bytes 442376 | tf_op jit(solution)/shard_map/ppermute | solution.py:202
  30.0 19.3 %all-to-all-start.1 = ((bf16[4,16,64,128]{3,2,1,0:T(8,128)(2,1)}), bf16[4,16,64,128]{3,2,1,0:T(8,128)(2,1)S(1)}, u32[]{:S(2)}, u32[]{:S(2)}) async-start(bf16[4,16,64,128]{3,2,1,0:T(8,128)(2,1)} %broadcast_in_dim.7), calls=%async_computation.1 | async-start | bytes 2097152 | tf_op jit(solution)/shard_map/all_to_all | solution.py:185
  34.3 8.6 %collective-permute-start.1 = (bf16[144,512]{1,0:T(8,128)(2,1)S(1)}, bf16[144,512]{1,0:T(8,128)(2,1)S(1)}, u32[]{:S(2)}, u32[]{:S(2)}) collective-permute-start(bf16[144,512]{1,0:T(8,128)(2,1)S(1)} %pad_maximum_fusion.refs_0_), channel_id=1, source_target_pairs={{0,64},{1,65},{64,0},{65,1},{2,66},{3,67},{66,2},{67,3},{4,68},{5,... | collective-permute-start | bytes 442376 | tf_op jit(solution)/shard_map/ppermute | solution.py:202
  38.9 7.9 %collective-permute-start.2 = (bf16[144,512]{1,0:T(8,128)(2,1)S(1)}, bf16[144,512]{1,0:T(8,128)(2,1)S(1)}, u32[]{:S(2)}, u32[]{:S(2)}) collective-permute-start(bf16[144,512]{1,0:T(8,128)(2,1)S(1)} %pad_maximum_fusion.refs_0_), channel_id=1, source_target_pairs={{0,65},{1,64},{64,1},{65,0},{2,67},{3,66},{66,3},{67,2},{4,69},{5,... | collective-permute-start | bytes 442376 | tf_op jit(solution)/shard_map/ppermute | solution.py:202
  49.3 28.6 %collective-permute-start.3 = (bf16[4,16,64,128]{3,2,1,0:T(8,128)(2,1)S(1)}, bf16[4,16,64,128]{3,2,1,0:T(8,128)(2,1)S(1)}, u32[]{:S(2)}, u32[]{:S(2)}) collective-permute-start(bf16[4,16,64,128]{3,2,1,0:T(8,128)(2,1)S(1)} %all-to-all-done.1.keys_ref), channel_id=1, source_target_pairs={{0,2},{2,0},{1,3},{3,1},{4,6},{6,4},{5,7},{7,5},{8,10},{10,8},{9,1... | collective-permute-start | bytes 3145736 | tf_op jit(solution)/shard_map/ppermute | solution.py:229

commit v3 on v2

--- a/solution.py
+++ b/solution.py
@@ -202,8 +202,8 @@
         return lax.ppermute(x, GROUP, [(i, i ^ step) for i in range(devices)])
 
     own = lax.dynamic_slice_in_dim(keys, lax.axis_index("head") * BLOCK, BLOCK, 0)
-    column, lines, near = lax.optimization_barrier((spread(own, ("yh", "zh")), lines, trade(lines, 1)))
-    own_keys = spread(column, "x")
+    column, lines, near = lax.optimization_barrier((spread(spread(own, "zh"), "yh"), lines, trade(lines, 1)))
+    own_keys = spread(column.reshape(-1, BLOCK, width), "x")
     across, along = trade(lines, 3), trade(lines, 2)
     all_queries = [lines, near, along, across]
 

time: 121 us -> 124 us (1.025)
  blocking collectives: 15.4 us -> 33.8 us
  starting transfers between devices: 32.1 us -> 22.8 us
  waiting for transfers between devices: 15.1 us -> 9.37 us
    all_to_all x1 -> x2, blocking collectives: 7.96 us -> 26.3 us  [spread(): return lax.all_to_all(copies, axes, 0, 0, tiled=True)]
    all_to_all x2, starting transfers between devices: 19.9 us -> 11.4 us  [spread(): return lax.all_to_all(copies, axes, 0, 0, tiled=True)]
    ppermute x3, waiting for transfers between devices: 12.6 us -> 8.43 us  [trade(): return lax.ppermute(x, GROUP, [(i, i ^ step) for i in range(devices)])]
    all_to_all x2, waiting for transfers between devices: 2.46 us -> 0.94 us  [spread(): return lax.all_to_all(copies, axes, 0, 0, tiled=True)]
where the time goes in v3:
time: 124 us
  Pallas kernels  54.6 us (44%)
  blocking collectives  33.8 us (27%)
  starting transfers between devices  22.8 us (18%)
  waiting for transfers between devices  9.37 us (8%)
  local copies, waits for them, and re-layouts  2.96 us (2%)
    pallas_call x2, Pallas kernels, score(): pl.pallas_call(functools.partial(score_kernel, members=members, heads=hea...  53.3 us
    all_to_all x2, blocking collectives, spread(): return lax.all_to_all(copies, axes, 0, 0, tiled=True)  26.3 us
    all_to_all x2, starting transfers between devices, spread(): return lax.all_to_all(copies, axes, 0, 0, tiled=True)  11.4 us
    ppermute x3, starting transfers between devices, trade(): return lax.ppermute(x, GROUP, [(i, i ^ step) for i in range(devices)])  9.54 us
    ppermute x3, waiting for transfers between devices, trade(): return lax.ppermute(x, GROUP, [(i, i ^ step) for i in range(devices)])  8.43 us
    all_to_all x1, blocking collectives, body(): mass = lax.all_to_all(mass, GROUP, 0, 0, tiled=True)  7.41 us
  transfers between devices with their start and end apart: 6, of which 5 were waited for; matrix products, arithmetic and copies ran while one was open for 0% of the time, Pallas kernels for 22%

profile of v3, /device:TPU:56, one launch (start us, length us, event | category | flops | bytes accessed | tf_op | source)
XLA Modules:
  0.0 123.7 jit_solution(8213473863632972246)
XLA Ops:
  0.0 0.8 copy-done
  0.8 18.5 %all_to_all.25 = bf16[4,64,128]{2,1,0:T(8,128)(2,1)S(1)} all-to-all(bf16[4,64,128]{2,1,0:T(8,128)(2,1)S(1)} %broadcast_in_dim.10), channel_id=1, replica_groups=mesh['yh'=4,'yl'=2,'zh'=4,'x'=4,'core'=2,'head'=2] {'zh'}, dimensions={0} | all-to-all | bytes 131072 | tf_op jit(solution)/shard_map/all_to_all | solution.py:185
  19.3 0.8 broadcast_in_dim.11
  20.0 7.1 %all-to-all-start.1 = ((bf16[4,4,64,128]{3,2,1,0:T(8,128)(2,1)}), bf16[4,4,64,128]{3,2,1,0:T(8,128)(2,1)S(1)}, u32[]{:S(2)}, u32[]{:S(2)}) async-start(bf16[4,4,64,128]{3,2,1,0:T(8,128)(2,1)} %broadcast_in_dim.11), calls=%async_computation.1 | async-start | bytes 524288 | tf_op jit(solution)/shard_map/all_to_all | solution.py:185
  27.1 0.1 copy.4
  27.4 3.2 %collective-permute-start = (bf16[144,512]{1,0:T(8,128)(2,1)S(1)}, bf16[144,512]{1,0:T(8,128)(2,1)S(1)}, u32[]{:S(2)}, u32[]{:S(2)}) collective-permute-start(bf16[144,512]{1,0:T(8,128)(2,1)S(1)} %pad_maximum_fusion.refs_0_), channel_id=1, source_target_pairs={{0,1},{1,0},{64,65},{65,64},{2,3},{3,2},{66,67},{67,66},{4,5},{5,4... | collective-permute-start | bytes 442376 | tf_op jit(solution)/shard_map/ppermute | solution.py:202
  30.6 3.8 %collective-permute-done.refs_1_ = bf16[144,512]{1,0:T(8,128)(2,1)S(1)} collective-permute-done((bf16[144,512]{1,0:T(8,128)(2,1)S(1)}, bf16[144,512]{1,0:T(8,128)(2,1)S(1)}, u32[]{:S(2)}, u32[]{:S(2)}) %collective-permute-start) | collective-permute-done | bytes 147488 | tf_op jit(solution)/shard_map/ppermute | solution.py:202
  34.4 0.2 all-to-all-done.1
  34.6 1.2 %broadcast_in_dim.13 = bf16[4,16,64,128]{3,2,1,0:T(8,128)(2,1)} broadcast(bf16[16,64,128]{2,1,0:T(8,128)(2,1)S(1)} %bitcast.14), dimensions={1,2,3} | broadcast | bytes 1310720 | tf_op jit(solution)/shard_map/broadcast_in_dim | solution.py:184
  35.9 4.3 %all-to-all-start.2 = ((bf16[4,16,64,128]{3,2,1,0:T(8,128)(2,1)}), bf16[4,16,64,128]{3,2,1,0:T(8,128)(2,1)S(1)}, u32[]{:S(2)}, u32[]{:S(2)}) async-start(bf16[4,16,64,128]{3,2,1,0:T(8,128)(2,1)} %broadcast_in_dim.13), calls=%async_computation.2 | async-start | bytes 2097152 | tf_op jit(solution)/shard_map/all_to_all | solution.py:185
  40.2 3.0 %collective-permute-start.1 = (bf16[144,512]{1,0:T(8,128)(2,1)S(1)}, bf16[144,512]{1,0:T(8,128)(2,1)S(1)}, u32[]{:S(2)}, u32[]{:S(2)}) collective-permute-start(bf16[144,512]{1,0:T(8,128)(2,1)S(1)} %pad_maximum_fusion.refs_0_), channel_id=1, source_target_pairs={{0,64},{1,65},{64,0},{65,1},{2,66},{3,67},{66,2},{67,3},{4,68},{5,... | collective-permute-start | bytes 442376 | tf_op jit(solution)/shard_map/ppermute | solution.py:202
  43.2 3.3 %collective-permute-start.2 = (bf16[144,512]{1,0:T(8,128)(2,1)S(1)}, bf16[144,512]{1,0:T(8,128)(2,1)S(1)}, u32[]{:S(2)}, u32[]{:S(2)}) collective-permute-start(bf16[144,512]{1,0:T(8,128)(2,1)S(1)} %pad_maximum_fusion.refs_0_), channel_id=1, source_target_pairs={{0,65},{1,64},{64,1},{65,0},{2,67},{3,66},{66,3},{67,2},{4,69},{5,... | collective-permute-start | bytes 442376 | tf_op jit(solution)/shard_map/ppermute | solution.py:202
  46.5 1.3 %collective-permute-done.1.refs_2_ = bf16[144,512]{1,0:T(8,128)(2,1)S(1)} collective-permute-done((bf16[144,512]{1,0:T(8,128)(2,1)S(1)}, bf16[144,512]{1,0:T(8,128)(2,1)S(1)}, u32[]{:S(2)}, u32[]{:S(2)}) %collective-permute-start.1) | collective-permute-done | bytes 147488 | tf_op jit(solution)/shard_map/ppermute | solution.py:202
  47.8 3.3 %collective-permute-done.2.refs_3_ = bf16[144,512]{1,0:T(8,128)(2,1)S(1)} collective-permute-done((bf16[144,512]{1,0:T(8,128)(2,1)S(1)}, bf16[144,512]{1,0:T(8,128)(2,1)S(1)}, u32[]{:S(2)}, u32[]{:S(2)}) %collective-permute-start.2) | collective-permute-done | bytes 147488 | tf_op jit(solution)/shard_map/ppermute | solution.py:202
  51.1 0.4 prepare.1
  51.5 0.7 all-to-all-done.2.keys_ref
  52.2 1.9 %collective-permute-start.3 = (bf16[4,16,64,128]{3,2,1,0:T(8,128)(2,1)S(1)}, bf16[4,16,64,128]{3,2,1,0:T(8,128)(2,1)S(1)}, u32[]{:S(2)}, u32[]{:S(2)}) collective-permute-start(bf16[4,16,64,128]{3,2,1,0:T(8,128)(2,1)S(1)} %all-to-all-done.2.keys_ref), channel_id=1, source_target_pairs={{0,2},{2,0},{1,3},{3,1},{4,6},{6,4},{5,7},{7,5},{8,10},{10,8},{9,1... | collective-permute-start | bytes 3145736 | tf_op jit(solution)/shard_map/ppermute | solution.py:229
  54.1 26.7 %score.2 = (f32[64,2048]{1,0:T(8,128)S(1)}, f32[2,2048]{1,0:T(2,128)S(1)}) custom-call(f32[8,128]{1,0:T(8,128)S(1)} %get-tuple-element.19.most_ref, s32[4,128]{1,0:T(4,128)S(1)} %get-tuple-element.20.starts_ref, bf16[256,2048]{1,0:T(8,128)(2,1)S(1)} %get-tuple-element.23.lines_ref, bf16[4,16,64,128]{3,2,1,0:T(8,128)(2,1)S(1)} %all-to-all-done.2.keys_ref), custom_call_target="tpu_custom_call" | custom-call | flops 2147483648 | bytes 8388608 | tf_op jit(solution)/shard_map/score/pallas_call | solution.py:232
  80.8 0.0 collective-permute-done.3.keys_ref
  80.8 26.7 %score.3 = (f32[64,2048]{1,0:T(8,128)S(1)}, f32[2,2048]{1,0:T(2,128)S(1)}) custom-call(f32[8,128]{1,0:T(8,128)S(1)} %get-tuple-element.19.most_ref, s32[4,128]{1,0:T(4,128)S(1)} %get-tuple-element.20.starts_ref, bf16[256,2048]{1,0:T(8,128)(2,1)S(1)} %get-tuple-element.23.lines_ref, bf16[4,16,64,128]{3,2,1,0:T(8,128)(2,1)S(1)} %collective-permute-done.3.keys_ref), custom_call_target="tpu_custom_call" | custom-call | flops 2147483648 | bytes 8388608 | tf_op jit(solution)/shard_map/score/pallas_call | solution.py:232
  107.5 7.9 %all_to_all.26.stat_ref = f32[4,4,2048]{2,1,0:T(4,128)S(1)} all-to-all(f32[4,4,2048]{2,1,0:T(4,128)S(1)} %broadcast_in_dim.14), channel_id=1, replica_groups=mesh['yh'=4,'yl'=2,'zh'=4,'x'=4,'core'=2,'head'=2] {'yl','head'}, dimensions={0} | all-to-all | bytes 262144 | tf_op jit(solution)/shard_map/all_to_all | solution.py:185
  115.4 0.1 mass.1
  115.5 7.4 %all_to_all.27.mass_ref = f32[4,2,2,16,128]{4,3,2,1,0:T(8,128)S(1)} all-to-all(f32[4,2,2,16,128]{4,3,2,1,0:T(8,128)S(1)} %bitcast.12), channel_id=1, replica_groups=mesh['yh'=4,'yl'=2,'zh'=4,'x'=4,'core'=2,'head'=2] {'yl','head'}, dimensions={0} | all-to-all | bytes 262144 | tf_op jit(solution)/shard_map/all_to_all | solution.py:267
  123.0 0.8 target.1
  (13 shorter events, 0.1 us)
Async XLA Ops:
  0.0 0.8 copy-start
  20.0 7.1 %copy-start.1 = (s32[128]{0:T(128)S(1)}, s32[128]{0:T(128)}, u32[]{:S(2)}) copy-start(s32[128]{0:T(128)} %param.5) | copy-start | bytes 1540
  20.0 7.1 %copy-start.2 = (bf16[128,4,128]{2,1,0:T(4,128)(2,1)S(1)}, bf16[128,4,128]{2,1,0:T(4,128)(2,1)}, u32[]{:S(2)}) copy-start(bf16[128,4,128]{2,1,0:T(4,128)(2,1)} %param.3) | copy-start | bytes 393220
  20.0 14.6 %all-to-all-start.1 = ((bf16[4,4,64,128]{3,2,1,0:T(8,128)(2,1)}), bf16[4,4,64,128]{3,2,1,0:T(8,128)(2,1)S(1)}, u32[]{:S(2)}, u32[]{:S(2)}) async-start(bf16[4,4,64,128]{3,2,1,0:T(8,128)(2,1)} %broadcast_in_dim.11), calls=%async_computation.1 | async-start | bytes 524288 | tf_op jit(solution)/shard_map/all_to_all | solution.py:185
  27.4 7.0 %collective-permute-start = (bf16[144,512]{1,0:T(8,128)(2,1)S(1)}, bf16[144,512]{1,0:T(8,128)(2,1)S(1)}, u32[]{:S(2)}, u32[]{:S(2)}) collective-permute-start(bf16[144,512]{1,0:T(8,128)(2,1)S(1)} %pad_maximum_fusion.refs_0_), channel_id=1, source_target_pairs={{0,1},{1,0},{64,65},{65,64},{2,3},{3,2},{66,67},{67,66},{4,5},{5,4... | collective-permute-start | bytes 442376 | tf_op jit(solution)/shard_map/ppermute | solution.py:202
  35.9 16.3 %all-to-all-start.2 = ((bf16[4,16,64,128]{3,2,1,0:T(8,128)(2,1)}), bf16[4,16,64,128]{3,2,1,0:T(8,128)(2,1)S(1)}, u32[]{:S(2)}, u32[]{:S(2)}) async-start(bf16[4,16,64,128]{3,2,1,0:T(8,128)(2,1)} %broadcast_in_dim.13), calls=%async_computation.2 | async-start | bytes 2097152 | tf_op jit(solution)/shard_map/all_to_all | solution.py:185
  40.2 7.7 %collective-permute-start.1 = (bf16[144,512]{1,0:T(8,128)(2,1)S(1)}, bf16[144,512]{1,0:T(8,128)(2,1)S(1)}, u32[]{:S(2)}, u32[]{:S(2)}) collective-permute-start(bf16[144,512]{1,0:T(8,128)(2,1)S(1)} %pad_maximum_fusion.refs_0_), channel_id=1, source_target_pairs={{0,64},{1,65},{64,0},{65,1},{2,66},{3,67},{66,2},{67,3},{4,68},{5,... | collective-permute-start | bytes 442376 | tf_op jit(solution)/shard_map/ppermute | solution.py:202
  43.2 7.9 %collective-permute-start.2 = (bf16[144,512]{1,0:T(8,128)(2,1)S(1)}, bf16[144,512]{1,0:T(8,128)(2,1)S(1)}, u32[]{:S(2)}, u32[]{:S(2)}) collective-permute-start(bf16[144,512]{1,0:T(8,128)(2,1)S(1)} %pad_maximum_fusion.refs_0_), channel_id=1, source_target_pairs={{0,65},{1,64},{64,1},{65,0},{2,67},{3,66},{66,3},{67,2},{4,69},{5,... | collective-permute-start | bytes 442376 | tf_op jit(solution)/shard_map/ppermute | solution.py:202
  52.2 28.6 %collective-permute-start.3 = (bf16[4,16,64,128]{3,2,1,0:T(8,128)(2,1)S(1)}, bf16[4,16,64,128]{3,2,1,0:T(8,128)(2,1)S(1)}, u32[]{:S(2)}, u32[]{:S(2)}) collective-permute-start(bf16[4,16,64,128]{3,2,1,0:T(8,128)(2,1)S(1)} %all-to-all-done.2.keys_ref), channel_id=1, source_target_pairs={{0,2},{2,0},{1,3},{3,1},{4,6},{6,4},{5,7},{7,5},{8,10},{10,8},{9,1... | collective-permute-start | bytes 3145736 | tf_op jit(solution)/shard_map/ppermute | solution.py:229

commit v4 on v2

--- a/solution.py
+++ b/solution.py
@@ -13,7 +13,6 @@
 CHUNK = 16
 LOW = -1e30
 SAFE = 60.0
-LOG2E = math.log2(math.e)
 
 
 def shard_of(index, low, core):
@@ -30,7 +29,7 @@
         source = mine ^ slot
         raw = q_ref[0:depth, :].astype(jnp.float32)
         most = jnp.maximum(most, jnp.max(jnp.sum(raw * raw, axis=0, keepdims=True)))
-        scaled = raw * (scale * LOG2E)
+        scaled = raw * scale
         high = scaled.astype(jnp.bfloat16)
         low = (scaled - high.astype(jnp.float32)).astype(jnp.bfloat16)
         at = pl.ds(pl.multiple_of(source * half, half), half)
@@ -41,8 +40,17 @@
     most_ref[...] = jnp.full_like(most_ref, most)
 
 
-def score_kernel(most_ref, starts_ref, lines_ref, keys_ref, sums_ref, stat_ref, *refs, members, heads, rows, scale, swap):
-    mask_ref, tile_ref, part_ref, top_ref = refs
+def merge(first, second):
+    top = jnp.maximum(first[0:1, :], second[0:1, :])
+    total = first[1:2, :] * jnp.exp(first[0:1, :] - top) + second[1:2, :] * jnp.exp(second[0:1, :] - top)
+    return top, total
+
+
+def score_kernel(most_ref, starts_ref, lines_ref, keys_ref, *refs, members, heads, rows, scale, swap):
+    if swap:
+        earlier_ref, sums_ref, stat_ref, merged_ref, mask_ref, part_ref, top_ref = refs
+    else:
+        sums_ref, stat_ref, mask_ref, part_ref, top_ref = refs
     group = lax.axis_index(PLACE)
     mine = lax.axis_index(GROUP)
     core = lax.axis_index("core")
@@ -89,17 +97,15 @@
         def one_chunk(chunk, carry):
             keys = chunk_keys(chunk)
             fill_mask(chunk, 1.0, 0.0)
-            tile_ref[0] = scores(keys, 0)
             for tile in range(members * width // pair):
                 at = tile * pair
-                if at + pair < members * width:
-                    tile_ref[(tile + 1) % 2] = scores(keys, at + pair)
+                result = scores(keys, at)
                 for block in range(CHUNK):
                     lines = slice(block * BLOCK, (block + 1) * BLOCK)
                     mask = mask_ref[at // width, lines, :]
                     for column in range(2):
-                        x = tile_ref[tile % 2, lines, column * rows : (column + 1) * rows]
-                        weights = jnp.exp2(x) * mask
+                        x = result[lines, column * rows : (column + 1) * rows]
+                        weights = jnp.exp(x) * mask
                         part_ref[2 * tile + column, block * 8 : block * 8 + 8, :] = jnp.sum(
                             weights.reshape(BLOCK // 8, 8, rows), axis=0
                         )
@@ -132,7 +138,7 @@
             top_ref[:, at] = jnp.maximum(top_ref[:, at], jnp.max(x, axis=0, keepdims=True))
 
         def add(chunk, at, x):
-            weights = jnp.where(x > 0.5 * LOW, jnp.exp2(jnp.minimum(x - top_ref[:, at], 0.0)), 0.0)
+            weights = jnp.where(x > 0.5 * LOW, jnp.exp(jnp.minimum(x - top_ref[:, at], 0.0)), 0.0)
             sums_ref[lines_of(chunk), at] = jnp.sum(weights.reshape(CHUNK, BLOCK, pair), axis=1)
 
         top_ref[...] = jnp.full_like(top_ref, LOW)
@@ -143,16 +149,16 @@
     top = jnp.where(safe, jnp.zeros_like(total), top_ref[...])
     stat_ref[0:1, :] = jnp.where(total > 0.0, top, LOW)
     stat_ref[1:2, :] = total
-
-
-def mass_kernel(own_ref, other_ref, stat_ref, mass_ref, *, members, heads, rows):
-    mine = lax.axis_index(GROUP)
-    tops = [stat_ref[:, 0, :], stat_ref[:, 2, :]]
-    top = jnp.max(jnp.maximum(*tops), axis=0, keepdims=True)
-    total = stat_ref[:, 1, :] * jnp.exp2(tops[0] - top) + stat_ref[:, 3, :] * jnp.exp2(tops[1] - top)
-    total = jnp.sum(total, axis=0, keepdims=True)
+    if swap:
+        merged_ref[0:1, :], merged_ref[1:2, :] = merge(stat_ref[...], earlier_ref[...])
+
+
+def mass_kernel(own_ref, other_ref, own_stat_ref, other_stat_ref, stat_ref, mass_ref, *, members, heads, rows):
+    top = jnp.max(stat_ref[:, 0, :], axis=0, keepdims=True)
+    total = jnp.sum(stat_ref[:, 1, :] * jnp.exp(stat_ref[:, 0, :] - top), axis=0, keepdims=True)
+    tops = (own_stat_ref[0:1, :], other_stat_ref[0:1, :])
     for side, sums_ref in enumerate((own_ref, other_ref)):
-        share = jnp.exp2(stat_ref[mine, 2 * side : 2 * side + 1, :] - top) / total
+        share = jnp.exp(tops[side] - top) / total
         for member in range(members):
             mass = None
             for head in range(heads):
@@ -228,18 +234,18 @@
     own_keys, query_lines = lax.optimization_barrier((own_keys, query_lines))
     other_keys = lax.ppermute(own_keys, "core", [(0, 1), (1, 0)])
 
-    def score(half_keys, swap):
+    stat_shape = jax.ShapeDtypeStruct((2, total_rows), jnp.float32)
+
+    def score(half_keys, *earlier):
         return pl.pallas_call(
-            functools.partial(score_kernel, members=members, heads=heads, rows=rows, scale=scale, swap=swap),
-            out_shape=(
-                jax.ShapeDtypeStruct((blocks, total_rows), jnp.float32),
-                jax.ShapeDtypeStruct((2, total_rows), jnp.float32),
+            functools.partial(
+                score_kernel, members=members, heads=heads, rows=rows, scale=scale, swap=len(earlier)
             ),
-            in_specs=[vmem] * 4,
-            out_specs=(vmem, vmem),
+            out_shape=(jax.ShapeDtypeStruct((blocks, total_rows), jnp.float32), stat_shape) + (stat_shape,) * len(earlier),
+            in_specs=[vmem] * (4 + len(earlier)),
+            out_specs=(vmem,) * (2 + len(earlier)),
             scratch_shapes=[
                 pltpu.VMEM((members, CHUNK * BLOCK, rows), jnp.float32),
-                pltpu.VMEM((2, CHUNK * BLOCK, 2 * rows), jnp.float32),
                 pltpu.VMEM((total_rows // rows, CHUNK * 8, rows), jnp.float32),
                 pltpu.VMEM((1, total_rows), jnp.float32),
             ],
@@ -250,19 +256,19 @@
                 transcendentals=blocks * BLOCK * total_rows,
             ),
             name="score",
-        )(most, starts, query_lines, half_keys)
-
-    own_sums, own_stat = score(own_keys, 0)
-    other_sums, other_stat = score(other_keys, 1)
-    stats = spread(jnp.concatenate([own_stat, other_stat], axis=0), GROUP)
+        )(most, starts, query_lines, half_keys, *earlier)
+
+    own_sums, own_stat = score(own_keys)
+    other_sums, other_stat, stat = score(other_keys, own_stat)
+    stats = spread(stat, GROUP)
     mass = pl.pallas_call(
         functools.partial(mass_kernel, members=members, heads=heads, rows=rows),
         out_shape=jax.ShapeDtypeStruct((members, blocks // 16, 2, 16, rows), jnp.float32),
-        in_specs=[vmem] * 3,
+        in_specs=[vmem] * 5,
         out_specs=vmem,
         compiler_params=params,
         name="mass",
-    )(own_sums, other_sums, stats)
+    )(own_sums, other_sums, own_stat, other_stat, stats)
     mass = mass.reshape(devices, blocks // 32, 2, 16, rows)
     mass = lax.all_to_all(mass, GROUP, 0, 0, tiled=True)
     return pl.pallas_call(

time: 121 us -> 123 us (1.017)
  Pallas kernels: 54.6 us -> 56.9 us
    pallas_call x2, Pallas kernels: 53.3 us -> 55.6 us  [score(): pl.pallas_call(functools.partial(score_kernel, members=members, heads=hea...]
  transfers between devices with their start and end apart: 6 -> 6, of which waited for: 5 -> 5; matrix products, arithmetic and copies ran while one was open for 0% -> 0% of each run, Pallas kernels for 22% -> 23%
where the time goes in v4:
time: 123 us
  Pallas kernels  56.9 us (46%)
  starting transfers between devices  32.1 us (26%)
  waiting for transfers between devices  15.1 us (12%)
  blocking collectives  14.9 us (12%)
  local copies, waits for them, and re-layouts  3.57 us (3%)
    pallas_call x2, Pallas kernels, score(): pl.pallas_call(functools.partial(score_kernel, members=members, heads=hea...  55.6 us
    all_to_all x2, starting transfers between devices, spread(): return lax.all_to_all(copies, axes, 0, 0, tiled=True)  19.9 us
    ppermute x3, waiting for transfers between devices, trade(): return lax.ppermute(x, GROUP, [(i, i ^ step) for i in range(devices)])  12.6 us
    ppermute x3, starting transfers between devices, trade(): return lax.ppermute(x, GROUP, [(i, i ^ step) for i in range(devices)])  10.3 us
    all_to_all x1, blocking collectives, body(): mass = lax.all_to_all(mass, GROUP, 0, 0, tiled=True)  7.58 us
    all_to_all x1, blocking collectives, spread(): return lax.all_to_all(copies, axes, 0, 0, tiled=True)  7.35 us
  transfers between devices with their start and end apart: 6, of which 5 were waited for; matrix products, arithmetic and copies ran while one was open for 0% of the time, Pallas kernels for 23%

profile of v4, /device:TPU:56, one launch (start us, length us, event | category | flops | bytes accessed | tf_op | source)
XLA Modules:
  0.0 122.7 jit_solution(1513877389358502153)
XLA Ops:
  0.0 0.8 copy-done
  0.8 0.8 broadcast_in_dim.6
  1.5 15.6 %all-to-all-start = ((bf16[16,64,128]{2,1,0:T(8,128)(2,1)}), bf16[16,64,128]{2,1,0:T(8,128)(2,1)S(1)}, u32[]{:S(2)}, u32[]{:S(2)}) async-start(bf16[16,64,128]{2,1,0:T(8,128)(2,1)} %broadcast_in_dim.6), calls=%async_computation | async-start | bytes 524288 | tf_op jit(solution)/shard_map/all_to_all | solution.py:191
  17.1 0.1 copy.4
  17.3 0.0 copy-start.1
  17.3 0.6 copy-done.1
  18.0 3.4 %collective-permute-start = (bf16[144,512]{1,0:T(8,128)(2,1)S(1)}, bf16[144,512]{1,0:T(8,128)(2,1)S(1)}, u32[]{:S(2)}, u32[]{:S(2)}) collective-permute-start(bf16[144,512]{1,0:T(8,128)(2,1)S(1)} %pad_maximum_fusion.refs_0_), channel_id=1, source_target_pairs={{0,1},{1,0},{64,65},{65,64},{2,3},{3,2},{66,67},{67,66},{4,5},{5,4... | collective-permute-start | bytes 442376 | tf_op jit(solution)/shard_map/ppermute | solution.py:208
  21.4 7.0 %collective-permute-done.refs_1_ = bf16[144,512]{1,0:T(8,128)(2,1)S(1)} collective-permute-done((bf16[144,512]{1,0:T(8,128)(2,1)S(1)}, bf16[144,512]{1,0:T(8,128)(2,1)S(1)}, u32[]{:S(2)}, u32[]{:S(2)}) %collective-permute-start) | collective-permute-done | bytes 147488 | tf_op jit(solution)/shard_map/ppermute | solution.py:208
  28.4 0.4 all-to-all-done
  28.7 1.2 %broadcast_in_dim.7 = bf16[4,16,64,128]{3,2,1,0:T(8,128)(2,1)} broadcast(bf16[16,64,128]{2,1,0:T(8,128)(2,1)S(1)} %all-to-all-done), dimensions={1,2,3} | broadcast | bytes 1310720 | tf_op jit(solution)/shard_map/broadcast_in_dim | solution.py:190
  30.0 4.3 %all-to-all-start.1 = ((bf16[4,16,64,128]{3,2,1,0:T(8,128)(2,1)}), bf16[4,16,64,128]{3,2,1,0:T(8,128)(2,1)S(1)}, u32[]{:S(2)}, u32[]{:S(2)}) async-start(bf16[4,16,64,128]{3,2,1,0:T(8,128)(2,1)} %broadcast_in_dim.7), calls=%async_computation.1 | async-start | bytes 2097152 | tf_op jit(solution)/shard_map/all_to_all | solution.py:191
  34.3 4.6 %collective-permute-start.1 = (bf16[144,512]{1,0:T(8,128)(2,1)S(1)}, bf16[144,512]{1,0:T(8,128)(2,1)S(1)}, u32[]{:S(2)}, u32[]{:S(2)}) collective-permute-start(bf16[144,512]{1,0:T(8,128)(2,1)S(1)} %pad_maximum_fusion.refs_0_), channel_id=1, source_target_pairs={{0,64},{1,65},{64,0},{65,1},{2,66},{3,67},{66,2},{67,3},{4,68},{5,... | collective-permute-start | bytes 442376 | tf_op jit(solution)/shard_map/ppermute | solution.py:208
  38.9 2.3 %collective-permute-start.2 = (bf16[144,512]{1,0:T(8,128)(2,1)S(1)}, bf16[144,512]{1,0:T(8,128)(2,1)S(1)}, u32[]{:S(2)}, u32[]{:S(2)}) collective-permute-start(bf16[144,512]{1,0:T(8,128)(2,1)S(1)} %pad_maximum_fusion.refs_0_), channel_id=1, source_target_pairs={{0,65},{1,64},{64,1},{65,0},{2,67},{3,66},{66,3},{67,2},{4,69},{5,... | collective-permute-start | bytes 442376 | tf_op jit(solution)/shard_map/ppermute | solution.py:208
  41.2 1.6 %collective-permute-done.1.refs_2_ = bf16[144,512]{1,0:T(8,128)(2,1)S(1)} collective-permute-done((bf16[144,512]{1,0:T(8,128)(2,1)S(1)}, bf16[144,512]{1,0:T(8,128)(2,1)S(1)}, u32[]{:S(2)}, u32[]{:S(2)}) %collective-permute-start.1) | collective-permute-done | bytes 147488 | tf_op jit(solution)/shard_map/ppermute | solution.py:208
  42.8 4.0 %collective-permute-done.2.refs_3_ = bf16[144,512]{1,0:T(8,128)(2,1)S(1)} collective-permute-done((bf16[144,512]{1,0:T(8,128)(2,1)S(1)}, bf16[144,512]{1,0:T(8,128)(2,1)S(1)}, u32[]{:S(2)}, u32[]{:S(2)}) %collective-permute-start.2) | collective-permute-done | bytes 147488 | tf_op jit(solution)/shard_map/ppermute | solution.py:208
  46.8 0.4 prepare.1
  47.2 2.1 %all-to-all-done.1.keys_ref = bf16[4,16,64,128]{3,2,1,0:T(8,128)(2,1)S(1)} async-done(((bf16[4,16,64,128]{3,2,1,0:T(8,128)(2,1)}), bf16[4,16,64,128]{3,2,1,0:T(8,128)(2,1)S(1)}, u32[]{:S(2)}, u32[]{:S(2)}) %all-to-all-start.1) | async-done | bytes 1048608 | tf_op jit(solution)/shard_map/all_to_all | solution.py:191
  49.3 1.9 %collective-permute-start.3 = (bf16[4,16,64,128]{3,2,1,0:T(8,128)(2,1)S(1)}, bf16[4,16,64,128]{3,2,1,0:T(8,128)(2,1)S(1)}, u32[]{:S(2)}, u32[]{:S(2)}) collective-permute-start(bf16[4,16,64,128]{3,2,1,0:T(8,128)(2,1)S(1)} %all-to-all-done.1.keys_ref), channel_id=1, source_target_pairs={{0,2},{2,0},{1,3},{3,1},{4,6},{6,4},{5,7},{7,5},{8,10},{10,8},{9,1... | collective-permute-start | bytes 3145736 | tf_op jit(solution)/shard_map/ppermute | solution.py:235
  51.2 27.8 %score.2 = (f32[64,2048]{1,0:T(8,128)S(1)}, f32[2,2048]{1,0:T(2,128)S(1)}) custom-call(f32[8,128]{1,0:T(8,128)S(1)} %get-tuple-element.20.most_ref, s32[4,128]{1,0:T(4,128)S(1)} %get-tuple-element.21.starts_ref, bf16[256,2048]{1,0:T(8,128)(2,1)S(1)} %get-tuple-element.24.lines_ref, bf16[4,16,64,128]{3,2,1,0:T(8,128)(2,1)S(1)} %all-to-all-done.1.keys_ref), custom_call_target="tpu_custom_call" | custom-call | flops 2147483648 | bytes 8388608 | tf_op jit(solution)/shard_map/score/pallas_call | solution.py:240
  79.0 27.8 %score.3 = (f32[64,2048]{1,0:T(8,128)S(1)}, f32[2,2048]{1,0:T(2,128)S(1)}, f32[2,2048]{1,0:T(2,128)S(1)}) custom-call(f32[8,128]{1,0:T(8,128)S(1)} %get-tuple-element.20.most_ref, s32[4,128]{1,0:T(4,128)S(1)} %get-tuple-element.21.starts_ref, bf16[256,2048]{1,0:T(8,128)(2,1)S(1)} %get-tuple-element.24.lines_ref, ...), custom_call_target="tpu_custom_call" | custom-call | flops 2147483648 | bytes 8388608 | tf_op jit(solution)/shard_map/score/pallas_call | solution.py:240
  106.9 7.3 %all_to_all.20.stat_ref = f32[4,2,2048]{2,1,0:T(2,128)S(1)} all-to-all(f32[4,2,2048]{2,1,0:T(2,128)S(1)} %broadcast_in_dim.8), channel_id=1, replica_groups=mesh['yh'=4,'yl'=2,'zh'=4,'x'=4,'core'=2,'head'=2] {'yl','head'}, dimensions={0} | all-to-all | bytes 131072 | tf_op jit(solution)/shard_map/all_to_all | solution.py:191
  114.2 0.1 mass.1
  114.3 7.6 %all_to_all.21.mass_ref = f32[4,2,2,16,128]{4,3,2,1,0:T(8,128)S(1)} all-to-all(f32[4,2,2,16,128]{4,3,2,1,0:T(8,128)S(1)} %bitcast.11), channel_id=1, replica_groups=mesh['yh'=4,'yl'=2,'zh'=4,'x'=4,'core'=2,'head'=2] {'yl','head'}, dimensions={0} | all-to-all | bytes 262144 | tf_op jit(solution)/shard_map/all_to_all | solution.py:273
  121.9 0.8 target.1
  (10 shorter events, 0.1 us)
Async XLA Ops:
  0.0 0.8 copy-start
  1.5 15.6 %copy-start.2 = (bf16[128,4,128]{2,1,0:T(4,128)(2,1)S(1)}, bf16[128,4,128]{2,1,0:T(4,128)(2,1)}, u32[]{:S(2)}) copy-start(bf16[128,4,128]{2,1,0:T(4,128)(2,1)} %param.3) | copy-start | bytes 393220
  1.5 27.2 %all-to-all-start = ((bf16[16,64,128]{2,1,0:T(8,128)(2,1)}), bf16[16,64,128]{2,1,0:T(8,128)(2,1)S(1)}, u32[]{:S(2)}, u32[]{:S(2)}) async-start(bf16[16,64,128]{2,1,0:T(8,128)(2,1)} %broadcast_in_dim.6), calls=%async_computation | async-start | bytes 524288 | tf_op jit(solution)/shard_map/all_to_all | solution.py:191
  17.3 0.7 copy-start.1
  18.0 10.4 %collective-permute-start = (bf16[144,512]{1,0:T(8,128)(2,1)S(1)}, bf16[144,512]{1,0:T(8,128)(2,1)S(1)}, u32[]{:S(2)}, u32[]{:S(2)}) collective-permute-start(bf16[144,512]{1,0:T(8,128)(2,1)S(1)} %pad_maximum_fusion.refs_0_), channel_id=1, source_target_pairs={{0,1},{1,0},{64,65},{65,64},{2,3},{3,2},{66,67},{67,66},{4,5},{5,4... | collective-permute-start | bytes 442376 | tf_op jit(solution)/shard_map/ppermute | solution.py:208
  30.0 19.3 %all-to-all-start.1 = ((bf16[4,16,64,128]{3,2,1,0:T(8,128)(2,1)}), bf16[4,16,64,128]{3,2,1,0:T(8,128)(2,1)S(1)}, u32[]{:S(2)}, u32[]{:S(2)}) async-start(bf16[4,16,64,128]{3,2,1,0:T(8,128)(2,1)} %broadcast_in_dim.7), calls=%async_computation.1 | async-start | bytes 2097152 | tf_op jit(solution)/shard_map/all_to_all | solution.py:191
  34.3 8.6 %collective-permute-start.1 = (bf16[144,512]{1,0:T(8,128)(2,1)S(1)}, bf16[144,512]{1,0:T(8,128)(2,1)S(1)}, u32[]{:S(2)}, u32[]{:S(2)}) collective-permute-start(bf16[144,512]{1,0:T(8,128)(2,1)S(1)} %pad_maximum_fusion.refs_0_), channel_id=1, source_target_pairs={{0,64},{1,65},{64,0},{65,1},{2,66},{3,67},{66,2},{67,3},{4,68},{5,... | collective-permute-start | bytes 442376 | tf_op jit(solution)/shard_map/ppermute | solution.py:208
  38.9 7.9 %collective-permute-start.2 = (bf16[144,512]{1,0:T(8,128)(2,1)S(1)}, bf16[144,512]{1,0:T(8,128)(2,1)S(1)}, u32[]{:S(2)}, u32[]{:S(2)}) collective-permute-start(bf16[144,512]{1,0:T(8,128)(2,1)S(1)} %pad_maximum_fusion.refs_0_), channel_id=1, source_target_pairs={{0,65},{1,64},{64,1},{65,0},{2,67},{3,66},{66,3},{67,2},{4,69},{5,... | collective-permute-start | bytes 442376 | tf_op jit(solution)/shard_map/ppermute | solution.py:208
  49.3 29.7 %collective-permute-start.3 = (bf16[4,16,64,128]{3,2,1,0:T(8,128)(2,1)S(1)}, bf16[4,16,64,128]{3,2,1,0:T(8,128)(2,1)S(1)}, u32[]{:S(2)}, u32[]{:S(2)}) collective-permute-start(bf16[4,16,64,128]{3,2,1,0:T(8,128)(2,1)S(1)} %all-to-all-done.1.keys_ref), channel_id=1, source_target_pairs={{0,2},{2,0},{1,3},{3,1},{4,6},{6,4},{5,7},{7,5},{8,10},{10,8},{9,1... | collective-permute-start | bytes 3145736 | tf_op jit(solution)/shard_map/ppermute | solution.py:235

commit v5 on v4

--- a/solution.py
+++ b/solution.py
@@ -12,6 +12,7 @@
 BLOCK = 64
 CHUNK = 16
 LOW = -1e30
+LOG2E = math.log2(math.e)
 SAFE = 60.0
 
 
@@ -29,7 +30,7 @@
         source = mine ^ slot
         raw = q_ref[0:depth, :].astype(jnp.float32)
         most = jnp.maximum(most, jnp.max(jnp.sum(raw * raw, axis=0, keepdims=True)))
-        scaled = raw * scale
+        scaled = raw * (scale * LOG2E)
         high = scaled.astype(jnp.bfloat16)
         low = (scaled - high.astype(jnp.float32)).astype(jnp.bfloat16)
         at = pl.ds(pl.multiple_of(source * half, half), half)
@@ -42,7 +43,7 @@
 
 def merge(first, second):
     top = jnp.maximum(first[0:1, :], second[0:1, :])
-    total = first[1:2, :] * jnp.exp(first[0:1, :] - top) + second[1:2, :] * jnp.exp(second[0:1, :] - top)
+    total = first[1:2, :] * jnp.exp2(first[0:1, :] - top) + second[1:2, :] * jnp.exp2(second[0:1, :] - top)
     return top, total
 
 
@@ -105,7 +106,7 @@
                     mask = mask_ref[at // width, lines, :]
                     for column in range(2):
                         x = result[lines, column * rows : (column + 1) * rows]
-                        weights = jnp.exp(x) * mask
+                        weights = jnp.exp2(x) * mask
                         part_ref[2 * tile + column, block * 8 : block * 8 + 8, :] = jnp.sum(
                             weights.reshape(BLOCK // 8, 8, rows), axis=0
                         )
@@ -138,7 +139,7 @@
             top_ref[:, at] = jnp.maximum(top_ref[:, at], jnp.max(x, axis=0, keepdims=True))
 
         def add(chunk, at, x):
-            weights = jnp.where(x > 0.5 * LOW, jnp.exp(jnp.minimum(x - top_ref[:, at], 0.0)), 0.0)
+            weights = jnp.where(x > 0.5 * LOW, jnp.exp2(jnp.minimum(x - top_ref[:, at], 0.0)), 0.0)
             sums_ref[lines_of(chunk), at] = jnp.sum(weights.reshape(CHUNK, BLOCK, pair), axis=1)
 
         top_ref[...] = jnp.full_like(top_ref, LOW)
@@ -155,10 +156,10 @@
 
 def mass_kernel(own_ref, other_ref, own_stat_ref, other_stat_ref, stat_ref, mass_ref, *, members, heads, rows):
     top = jnp.max(stat_ref[:, 0, :], axis=0, keepdims=True)
-    total = jnp.sum(stat_ref[:, 1, :] * jnp.exp(stat_ref[:, 0, :] - top), axis=0, keepdims=True)
+    total = jnp.sum(stat_ref[:, 1, :] * jnp.exp2(stat_ref[:, 0, :] - top), axis=0, keepdims=True)
     tops = (own_stat_ref[0:1, :], other_stat_ref[0:1, :])
     for side, sums_ref in enumerate((own_ref, other_ref)):
-        share = jnp.exp(tops[side] - top) / total
+        share = jnp.exp2(tops[side] - top) / total
         for member in range(members):
             mass = None
             for head in range(heads):
@@ -208,10 +209,9 @@
         return lax.ppermute(x, GROUP, [(i, i ^ step) for i in range(devices)])
 
     own = lax.dynamic_slice_in_dim(keys, lax.axis_index("head") * BLOCK, BLOCK, 0)
-    column, lines, near = lax.optimization_barrier((spread(own, ("yh", "zh")), lines, trade(lines, 1)))
+    column, lines = lax.optimization_barrier((spread(own, ("yh", "zh")), lines))
     own_keys = spread(column, "x")
-    across, along = trade(lines, 3), trade(lines, 2)
-    all_queries = [lines, near, along, across]
+    all_queries = [lines, trade(lines, 1), trade(lines, 2), trade(lines, 3)]
 
     total_rows = members * heads * rows
     vmem = pl.BlockSpec(memory_space=pltpu.VMEM)

time: 123 us -> 121 us (0.984)
  Pallas kernels: 56.9 us -> 54.6 us
    ppermute x3, waiting for transfers between devices: 12.6 us -> 4.03 us  [trade(): return lax.ppermute(x, GROUP, [(i, i ^ step) for i in range(devices)])]
    all_to_all x2, waiting for transfers between devices: 2.46 us -> 10.7 us  [spread(): return lax.all_to_all(copies, axes, 0, 0, tiled=True)]
    pallas_call x2, Pallas kernels: 55.6 us -> 53.4 us  [score(): pl.pallas_call(functools.partial(score_kernel, members=members, heads=hea...]
  transfers between devices with their start and end apart: 6 -> 6, of which waited for: 5 -> 3; matrix products, arithmetic and copies ran while one was open for 0% -> 0% of each run, Pallas kernels for 23% -> 22%
where the time goes in v5:
time: 121 us; the launch traced here: 120 us
  Pallas kernels  54.6 us (45%)
  starting transfers between devices  31.7 us (26%)
  blocking collectives  15.5 us (13%)
  waiting for transfers between devices  14.8 us (12%)
  local copies, waits for them, and re-layouts  3.57 us (3%)
    pallas_call x2, Pallas kernels, score(): pl.pallas_call(functools.partial(score_kernel, members=members, heads=hea...  53.4 us
    all_to_all x2, starting transfers between devices, spread(): return lax.all_to_all(copies, axes, 0, 0, tiled=True)  19.9 us
    all_to_all x2, waiting for transfers between devices, spread(): return lax.all_to_all(copies, axes, 0, 0, tiled=True)  10.7 us
    ppermute x3, starting transfers between devices, trade(): return lax.ppermute(x, GROUP, [(i, i ^ step) for i in range(devices)])  9.93 us
    all_to_all x1, blocking collectives, spread(): return lax.all_to_all(copies, axes, 0, 0, tiled=True)  7.93 us
    all_to_all x1, blocking collectives, body(): mass = lax.all_to_all(mass, GROUP, 0, 0, tiled=True)  7.58 us
    ppermute x3, waiting for transfers between devices, trade(): return lax.ppermute(x, GROUP, [(i, i ^ step) for i in range(devices)])  4.03 us
  transfers between devices with their start and end apart: 6, of which 3 were waited for; matrix products, arithmetic and copies ran while one was open for 0% of the time, Pallas kernels for 22%

profile of v5, /device:TPU:56, one launch (start us, length us, event | category | flops | bytes accessed | tf_op | source)
XLA Modules:
  0.0 120.4 jit_solution(15953565754917697858)
XLA Ops:
  0.0 0.8 copy-done
  0.8 0.8 broadcast_in_dim.6
  1.5 15.6 %all-to-all-start = ((bf16[16,64,128]{2,1,0:T(8,128)(2,1)}), bf16[16,64,128]{2,1,0:T(8,128)(2,1)S(1)}, u32[]{:S(2)}, u32[]{:S(2)}) async-start(bf16[16,64,128]{2,1,0:T(8,128)(2,1)} %broadcast_in_dim.6), calls=%async_computation | async-start | bytes 524288 | tf_op jit(solution)/shard_map/all_to_all | solution.py:192
  17.1 0.1 copy.4
  17.3 0.0 copy-start.1
  17.3 0.6 copy-done.1
  18.0 10.7 %all-to-all-done = bf16[16,64,128]{2,1,0:T(8,128)(2,1)S(1)} async-done(((bf16[16,64,128]{2,1,0:T(8,128)(2,1)}), bf16[16,64,128]{2,1,0:T(8,128)(2,1)S(1)}, u32[]{:S(2)}, u32[]{:S(2)}) %all-to-all-start) | async-done | bytes 262176 | tf_op jit(solution)/shard_map/all_to_all | solution.py:192
  28.7 1.2 %broadcast_in_dim.7 = bf16[4,16,64,128]{3,2,1,0:T(8,128)(2,1)} broadcast(bf16[16,64,128]{2,1,0:T(8,128)(2,1)S(1)} %all-to-all-done), dimensions={1,2,3} | broadcast | bytes 1310720 | tf_op jit(solution)/shard_map/broadcast_in_dim | solution.py:191
  29.9 4.3 %all-to-all-start.1 = ((bf16[4,16,64,128]{3,2,1,0:T(8,128)(2,1)}), bf16[4,16,64,128]{3,2,1,0:T(8,128)(2,1)S(1)}, u32[]{:S(2)}, u32[]{:S(2)}) async-start(bf16[4,16,64,128]{3,2,1,0:T(8,128)(2,1)} %broadcast_in_dim.7), calls=%async_computation.1 | async-start | bytes 2097152 | tf_op jit(solution)/shard_map/all_to_all | solution.py:192
  34.2 5.0 %collective-permute-start.2 = (bf16[144,512]{1,0:T(8,128)(2,1)S(1)}, bf16[144,512]{1,0:T(8,128)(2,1)S(1)}, u32[]{:S(2)}, u32[]{:S(2)}) collective-permute-start(bf16[144,512]{1,0:T(8,128)(2,1)S(1)} %pad_maximum_fusion.refs_0_), channel_id=1, source_target_pairs={{0,65},{1,64},{64,1},{65,0},{2,67},{3,66},{66,3},{67,2},{4,69},{5,... | collective-permute-start | bytes 442376 | tf_op jit(solution)/shard_map/ppermute | solution.py:209
  39.3 1.9 %collective-permute-start.1 = (bf16[144,512]{1,0:T(8,128)(2,1)S(1)}, bf16[144,512]{1,0:T(8,128)(2,1)S(1)}, u32[]{:S(2)}, u32[]{:S(2)}) collective-permute-start(bf16[144,512]{1,0:T(8,128)(2,1)S(1)} %pad_maximum_fusion.refs_0_), channel_id=1, source_target_pairs={{0,64},{1,65},{64,0},{65,1},{2,66},{3,67},{66,2},{67,3},{4,68},{5,... | collective-permute-start | bytes 442376 | tf_op jit(solution)/shard_map/ppermute | solution.py:209
  41.2 3.0 %collective-permute-start = (bf16[144,512]{1,0:T(8,128)(2,1)S(1)}, bf16[144,512]{1,0:T(8,128)(2,1)S(1)}, u32[]{:S(2)}, u32[]{:S(2)}) collective-permute-start(bf16[144,512]{1,0:T(8,128)(2,1)S(1)} %pad_maximum_fusion.refs_0_), channel_id=1, source_target_pairs={{0,1},{1,0},{64,65},{65,64},{2,3},{3,2},{66,67},{67,66},{4,5},{5,4... | collective-permute-start | bytes 442376 | tf_op jit(solution)/shard_map/ppermute | solution.py:209
  44.2 0.0 collective-permute-done.2.refs_3_
  44.2 2.1 %collective-permute-done.1.refs_2_ = bf16[144,512]{1,0:T(8,128)(2,1)S(1)} collective-permute-done((bf16[144,512]{1,0:T(8,128)(2,1)S(1)}, bf16[144,512]{1,0:T(8,128)(2,1)S(1)}, u32[]{:S(2)}, u32[]{:S(2)}) %collective-permute-start.1) | collective-permute-done | bytes 147488 | tf_op jit(solution)/shard_map/ppermute | solution.py:209
  46.3 1.9 %collective-permute-done.refs_1_ = bf16[144,512]{1,0:T(8,128)(2,1)S(1)} collective-permute-done((bf16[144,512]{1,0:T(8,128)(2,1)S(1)}, bf16[144,512]{1,0:T(8,128)(2,1)S(1)}, u32[]{:S(2)}, u32[]{:S(2)}) %collective-permute-start) | collective-permute-done | bytes 147488 | tf_op jit(solution)/shard_map/ppermute | solution.py:209
  48.2 0.4 prepare.1
  48.6 1.9 %collective-permute-start.3 = (bf16[4,16,64,128]{3,2,1,0:T(8,128)(2,1)S(1)}, bf16[4,16,64,128]{3,2,1,0:T(8,128)(2,1)S(1)}, u32[]{:S(2)}, u32[]{:S(2)}) collective-permute-start(bf16[4,16,64,128]{3,2,1,0:T(8,128)(2,1)S(1)} %all-to-all-done.1.keys_ref), channel_id=1, source_target_pairs={{0,2},{2,0},{1,3},{3,1},{4,6},{6,4},{5,7},{7,5},{8,10},{10,8},{9,1... | collective-permute-start | bytes 3145736 | tf_op jit(solution)/shard_map/ppermute | solution.py:235
  50.5 26.7 %score.2 = (f32[64,2048]{1,0:T(8,128)S(1)}, f32[2,2048]{1,0:T(2,128)S(1)}) custom-call(f32[8,128]{1,0:T(8,128)S(1)} %get-tuple-element.18.most_ref, s32[4,128]{1,0:T(4,128)S(1)} %get-tuple-element.19.starts_ref, bf16[256,2048]{1,0:T(8,128)(2,1)S(1)} %get-tuple-element.22.lines_ref, bf16[4,16,64,128]{3,2,1,0:T(8,128)(2,1)S(1)} %all-to-all-done.1.keys_ref), custom_call_target="tpu_custom_call" | custom-call | flops 2147483648 | bytes 8388608 | tf_op jit(solution)/shard_map/score/pallas_call | solution.py:240
  77.2 0.0 collective-permute-done.3.keys_ref
  77.2 26.7 %score.3 = (f32[64,2048]{1,0:T(8,128)S(1)}, f32[2,2048]{1,0:T(2,128)S(1)}, f32[2,2048]{1,0:T(2,128)S(1)}) custom-call(f32[8,128]{1,0:T(8,128)S(1)} %get-tuple-element.18.most_ref, s32[4,128]{1,0:T(4,128)S(1)} %get-tuple-element.19.starts_ref, bf16[256,2048]{1,0:T(8,128)(2,1)S(1)} %get-tuple-element.22.lines_ref, ...), custom_call_target="tpu_custom_call" | custom-call | flops 2147483648 | bytes 8388608 | tf_op jit(solution)/shard_map/score/pallas_call | solution.py:240
  104.0 7.9 %all_to_all.20.stat_ref = f32[4,2,2048]{2,1,0:T(2,128)S(1)} all-to-all(f32[4,2,2048]{2,1,0:T(2,128)S(1)} %broadcast_in_dim.8), channel_id=1, replica_groups=mesh['yh'=4,'yl'=2,'zh'=4,'x'=4,'core'=2,'head'=2] {'yl','head'}, dimensions={0} | all-to-all | bytes 131072 | tf_op jit(solution)/shard_map/all_to_all | solution.py:192
  111.9 0.1 mass.1
  112.0 7.6 %all_to_all.21.mass_ref = f32[4,2,2,16,128]{4,3,2,1,0:T(8,128)S(1)} all-to-all(f32[4,2,2,16,128]{4,3,2,1,0:T(8,128)S(1)} %bitcast.11), channel_id=1, replica_groups=mesh['yh'=4,'yl'=2,'zh'=4,'x'=4,'core'=2,'head'=2] {'yl','head'}, dimensions={0} | all-to-all | bytes 262144 | tf_op jit(solution)/shard_map/all_to_all | solution.py:273
  119.6 0.8 target.1
  (10 shorter events, 0.1 us)
Async XLA Ops:
  0.0 0.8 copy-start
  1.5 15.6 %copy-start.2 = (bf16[128,4,128]{2,1,0:T(4,128)(2,1)S(1)}, bf16[128,4,128]{2,1,0:T(4,128)(2,1)}, u32[]{:S(2)}) copy-start(bf16[128,4,128]{2,1,0:T(4,128)(2,1)} %param.3) | copy-start | bytes 393220
  1.5 27.2 %all-to-all-start = ((bf16[16,64,128]{2,1,0:T(8,128)(2,1)}), bf16[16,64,128]{2,1,0:T(8,128)(2,1)S(1)}, u32[]{:S(2)}, u32[]{:S(2)}) async-start(bf16[16,64,128]{2,1,0:T(8,128)(2,1)} %broadcast_in_dim.6), calls=%async_computation | async-start | bytes 524288 | tf_op jit(solution)/shard_map/all_to_all | solution.py:192
  17.3 0.7 copy-start.1
  29.9 18.6 %all-to-all-start.1 = ((bf16[4,16,64,128]{3,2,1,0:T(8,128)(2,1)}), bf16[4,16,64,128]{3,2,1,0:T(8,128)(2,1)S(1)}, u32[]{:S(2)}, u32[]{:S(2)}) async-start(bf16[4,16,64,128]{3,2,1,0:T(8,128)(2,1)} %broadcast_in_dim.7), calls=%async_computation.1 | async-start | bytes 2097152 | tf_op jit(solution)/shard_map/all_to_all | solution.py:192
  34.2 10.0 %collective-permute-start.2 = (bf16[144,512]{1,0:T(8,128)(2,1)S(1)}, bf16[144,512]{1,0:T(8,128)(2,1)S(1)}, u32[]{:S(2)}, u32[]{:S(2)}) collective-permute-start(bf16[144,512]{1,0:T(8,128)(2,1)S(1)} %pad_maximum_fusion.refs_0_), channel_id=1, source_target_pairs={{0,65},{1,64},{64,1},{65,0},{2,67},{3,66},{66,3},{67,2},{4,69},{5,... | collective-permute-start | bytes 442376 | tf_op jit(solution)/shard_map/ppermute | solution.py:209
  39.3 7.0 %collective-permute-start.1 = (bf16[144,512]{1,0:T(8,128)(2,1)S(1)}, bf16[144,512]{1,0:T(8,128)(2,1)S(1)}, u32[]{:S(2)}, u32[]{:S(2)}) collective-permute-start(bf16[144,512]{1,0:T(8,128)(2,1)S(1)} %pad_maximum_fusion.refs_0_), channel_id=1, source_target_pairs={{0,64},{1,65},{64,0},{65,1},{2,66},{3,67},{66,2},{67,3},{4,68},{5,... | collective-permute-start | bytes 442376 | tf_op jit(solution)/shard_map/ppermute | solution.py:209
  41.2 7.0 %collective-permute-start = (bf16[144,512]{1,0:T(8,128)(2,1)S(1)}, bf16[144,512]{1,0:T(8,128)(2,1)S(1)}, u32[]{:S(2)}, u32[]{:S(2)}) collective-permute-start(bf16[144,512]{1,0:T(8,128)(2,1)S(1)} %pad_maximum_fusion.refs_0_), channel_id=1, source_target_pairs={{0,1},{1,0},{64,65},{65,64},{2,3},{3,2},{66,67},{67,66},{4,5},{5,4... | collective-permute-start | bytes 442376 | tf_op jit(solution)/shard_map/ppermute | solution.py:209
  48.6 28.6 %collective-permute-start.3 = (bf16[4,16,64,128]{3,2,1,0:T(8,128)(2,1)S(1)}, bf16[4,16,64,128]{3,2,1,0:T(8,128)(2,1)S(1)}, u32[]{:S(2)}, u32[]{:S(2)}) collective-permute-start(bf16[4,16,64,128]{3,2,1,0:T(8,128)(2,1)S(1)} %all-to-all-done.1.keys_ref), channel_id=1, source_target_pairs={{0,2},{2,0},{1,3},{3,1},{4,6},{6,4},{5,7},{7,5},{8,10},{10,8},{9,1... | collective-permute-start | bytes 3145736 | tf_op jit(solution)/shard_map/ppermute | solution.py:235

commit v6 on v5

--- a/solution.py
+++ b/solution.py
@@ -20,25 +20,53 @@
     return index // 16 * 64 + low * 32 + index % 16 * 2 + core
 
 
-def prepare_kernel(*refs, scale, rows):
-    *q_refs, lines_ref, starts_ref, most_ref = refs
+def prepare_kernel(*refs, scale, rows, heads):
+    *q_refs, lines_ref, starts_ref, places_ref, order_ref, most_ref, raw_ref, aux_ref = refs
     mine = lax.axis_index(GROUP)
     depth = lines_ref.shape[0] // 2
-    half = lines_ref.shape[1] // len(q_refs)
+    total = 2 * rows
     most = jnp.float32(0.0)
     for slot, q_ref in enumerate(q_refs):
         source = mine ^ slot
-        raw = q_ref[0:depth, :].astype(jnp.float32)
-        most = jnp.maximum(most, jnp.max(jnp.sum(raw * raw, axis=0, keepdims=True)))
-        scaled = raw * (scale * LOG2E)
-        high = scaled.astype(jnp.bfloat16)
-        low = (scaled - high.astype(jnp.float32)).astype(jnp.bfloat16)
-        at = pl.ds(pl.multiple_of(source * half, half), half)
-        lines_ref[0:depth, at] = high
-        lines_ref[depth : 2 * depth, at] = low
-        digits = q_ref[depth : depth + 16, 0:rows].astype(jnp.float32)
-        starts_ref[pl.ds(source, 1), :] = (digits[0:1, :] * 256.0 + digits[1:2, :]).astype(jnp.int32)
+        raw = q_ref[0:depth, :]
+        wide = raw.astype(jnp.float32)
+        most = jnp.maximum(most, jnp.max(jnp.sum(wide * wide, axis=0, keepdims=True)))
+        raw_ref[source] = raw
+        aux_ref[source] = q_ref[depth : depth + 16, 0:rows]
     most_ref[...] = jnp.full_like(most_ref, most)
+
+    aux = jnp.concatenate([aux_ref[0], aux_ref[2]], axis=1).astype(jnp.float32)
+    row = lax.broadcasted_iota(jnp.int32, (1, total), 1).astype(jnp.float32)
+    start = aux[0:1, :] * 256.0 + aux[1:2, :]
+    key = jnp.broadcast_to(start * float(total) + row, (total, total))
+    rank = jnp.sum(jnp.where(key.T < key, 1.0, 0.0), axis=0, keepdims=True)
+    line = lax.broadcasted_iota(jnp.int32, (total, total), 0).astype(jnp.float32)
+    order = jnp.where(rank == line, 1.0, 0.0).astype(jnp.bfloat16)
+    order_ref[...] = order
+
+    def in_order(values):
+        return lax.dot_general(values, order, (((1,), (1,)), ((), ())), preferred_element_type=jnp.float32)
+
+    spots = in_order(jnp.where(lax.broadcasted_iota(jnp.int32, aux.shape, 0) == 2, row, aux).astype(jnp.bfloat16))
+    group = lax.axis_index(PLACE)
+    core = lax.axis_index("core")
+    for half in range(2):
+        here = spots[:, half * rows : (half + 1) * rows]
+        index = here[2:3, :].astype(jnp.int32)
+        starts_ref[half : half + 1, :] = (here[0:1, :] * 256.0 + here[1:2, :]).astype(jnp.int32)
+        places_ref[half : half + 1, :] = shard_of(group, index // rows, core) * rows + index % rows
+
+    for head in range(heads):
+        source = head // 4
+        lane = slice(head % 4 * rows, (head % 4 + 1) * rows)
+        x = in_order(jnp.concatenate([raw_ref[source, :, lane], raw_ref[2 + source, :, lane]], axis=1))
+        x = x * (scale * LOG2E)
+        high = x.astype(jnp.bfloat16)
+        low = (x - high.astype(jnp.float32)).astype(jnp.bfloat16)
+        for half in range(2):
+            at = slice((half * heads + head) * rows, (half * heads + head + 1) * rows)
+            lines_ref[0:depth, at] = high[:, half * rows : (half + 1) * rows]
+            lines_ref[depth : 2 * depth, at] = low[:, half * rows : (half + 1) * rows]
 
 
 def merge(first, second):
@@ -47,7 +75,7 @@
     return top, total
 
 
-def score_kernel(most_ref, starts_ref, lines_ref, keys_ref, *refs, members, heads, rows, scale, swap):
+def score_kernel(most_ref, starts_ref, places_ref, lines_ref, keys_ref, *refs, members, heads, rows, scale, swap):
     if swap:
         earlier_ref, sums_ref, stat_ref, merged_ref, mask_ref, part_ref, top_ref = refs
     else:
@@ -65,10 +93,12 @@
     safe = jnp.max(most_ref[...]) * longest * (scale * scale) <= SAFE * SAFE
     sums_ref[...] = jnp.zeros_like(sums_ref)
 
-    starts = [starts_ref[2 * member : 2 * member + 1, :] for member in range(members)]
-    first_start = jnp.min(functools.reduce(jnp.minimum, starts))
+    reach = rows * 32
+    parity = mine // 2
     last_chunk = group // CHUNK
-    first_chunk = jnp.minimum(first_start // (rows * 64), last_chunk)
+    starts = [starts_ref[half : half + 1, :] for half in range(members)]
+    places = [places_ref[half : half + 1, :] for half in range(members)]
+    first_chunks = [(starts_ref[half, 0] // reach - parity + 1) // 2 for half in range(members)]
 
     def chunk_keys(chunk):
         blocks = [keys_ref[column, chunk * 4 + step] for step in range(4) for column in range(4)]
@@ -76,16 +106,12 @@
         return jnp.concatenate([keys, keys], axis=1)
 
     line = lax.broadcasted_iota(jnp.int32, (BLOCK, rows), 0)
-    places = [
-        shard_of(group, member, core) * rows + lax.broadcasted_iota(jnp.int32, (1, rows), 1) for member in range(members)
-    ]
-
-    def fill_mask(chunk, inside, outside):
+
+    def fill_mask(chunk, half, inside, outside):
         for block in range(CHUNK):
-            base = (shard_of(chunk * CHUNK + block, mine // 2, side) * 2 + mine % 2) * BLOCK
-            for member in range(members):
-                allowed = (line >= starts[member] - base) & (line <= places[member] - base)
-                mask_ref[member, block * BLOCK : (block + 1) * BLOCK, :] = jnp.where(allowed, inside, outside)
+            base = (shard_of(chunk * CHUNK + block, parity, side) * 2 + mine % 2) * BLOCK
+            allowed = (line >= starts[half] - base) & (line <= places[half] - base)
+            mask_ref[half, block * BLOCK : (block + 1) * BLOCK, :] = jnp.where(allowed, inside, outside)
 
     def scores(keys, at):
         return jnp.dot(keys, lines_ref[:, pl.ds(at, pair)], preferred_element_type=jnp.float32)
@@ -93,17 +119,19 @@
     def lines_of(chunk):
         return pl.ds(pl.multiple_of(chunk * CHUNK, CHUNK), CHUNK)
 
-    @pl.when(safe)
-    def _():
+    def each_chunk(half, visit):
+        lax.fori_loop(first_chunks[half], last_chunk + 1, visit, 0)
+
+    def some_tiles(half):
         def one_chunk(chunk, carry):
             keys = chunk_keys(chunk)
-            fill_mask(chunk, 1.0, 0.0)
-            for tile in range(members * width // pair):
+            fill_mask(chunk, half, 1.0, 0.0)
+            for tile in range(half * width // pair, (half + 1) * width // pair):
                 at = tile * pair
                 result = scores(keys, at)
                 for block in range(CHUNK):
                     lines = slice(block * BLOCK, (block + 1) * BLOCK)
-                    mask = mask_ref[at // width, lines, :]
+                    mask = mask_ref[half, lines, :]
                     for column in range(2):
                         x = result[lines, column * rows : (column + 1) * rows]
                         weights = jnp.exp2(x) * mask
@@ -117,21 +145,26 @@
                     sums_ref[lines_of(chunk), at + column * rows : at + (column + 1) * rows] = total
             return carry
 
-        lax.fori_loop(first_chunk, last_chunk + 1, one_chunk, 0)
-
-    def each_tile(visit):
+        each_chunk(half, one_chunk)
+
+    @pl.when(safe)
+    def _():
+        for half in range(members):
+            some_tiles(half)
+
+    def each_tile(half, visit):
         def one_chunk(chunk, carry):
-            fill_mask(chunk, 0.0, LOW)
+            fill_mask(chunk, half, 0.0, LOW)
 
             def one_tile(tile, carry):
-                at = pl.multiple_of(tile * pair, pair)
-                mask = mask_ref[at // width]
+                at = pl.multiple_of(half * width + tile * pair, pair)
+                mask = mask_ref[half]
                 visit(chunk, pl.ds(at, pair), scores(chunk_keys(chunk), at) + jnp.concatenate([mask, mask], axis=1))
                 return carry
 
-            return lax.fori_loop(0, members * width // pair, one_tile, carry)
-
-        lax.fori_loop(first_chunk, last_chunk + 1, one_chunk, 0)
+            return lax.fori_loop(0, width // pair, one_tile, carry)
+
+        each_chunk(half, one_chunk)
 
     @pl.when(jnp.logical_not(safe))
     def _():
@@ -143,8 +176,9 @@
             sums_ref[lines_of(chunk), at] = jnp.sum(weights.reshape(CHUNK, BLOCK, pair), axis=1)
 
         top_ref[...] = jnp.full_like(top_ref, LOW)
-        each_tile(raise_top)
-        each_tile(add)
+        for half in range(members):
+            each_tile(half, raise_top)
+            each_tile(half, add)
 
     total = jnp.sum(sums_ref[...], axis=0, keepdims=True)
     top = jnp.where(safe, jnp.zeros_like(total), top_ref[...])
@@ -154,20 +188,31 @@
         merged_ref[0:1, :], merged_ref[1:2, :] = merge(stat_ref[...], earlier_ref[...])
 
 
-def mass_kernel(own_ref, other_ref, own_stat_ref, other_stat_ref, stat_ref, mass_ref, *, members, heads, rows):
+def mass_kernel(own_ref, other_ref, own_stat_ref, other_stat_ref, stat_ref, order_ref, mass_ref, *, members, heads, rows):
     top = jnp.max(stat_ref[:, 0, :], axis=0, keepdims=True)
     total = jnp.sum(stat_ref[:, 1, :] * jnp.exp2(stat_ref[:, 0, :] - top), axis=0, keepdims=True)
     tops = (own_stat_ref[0:1, :], other_stat_ref[0:1, :])
+    order = order_ref[...]
     for side, sums_ref in enumerate((own_ref, other_ref)):
         share = jnp.exp2(tops[side] - top) / total
-        for member in range(members):
+        halves = []
+        for half in range(members):
             mass = None
             for head in range(heads):
-                at = (member * heads + head) * rows
+                at = (half * heads + head) * rows
                 term = sums_ref[:, at : at + rows] * share[:, at : at + rows]
                 mass = term if mass is None else mass + term
-            for run in range(mass_ref.shape[1]):
-                mass_ref[member, run, side] = mass[run * 16 : run * 16 + 16, :]
+            halves.append(mass)
+        rest = jnp.concatenate(halves, axis=1)
+        mass = None
+        for _ in range(3):
+            term = rest.astype(jnp.bfloat16)
+            rest = rest - term.astype(jnp.float32)
+            back = jnp.dot(term, order, preferred_element_type=jnp.float32)
+            mass = back if mass is None else mass + back
+        for member in range(members):
+            for level in range(mass_ref.shape[1]):
+                mass_ref[member, level, side] = mass[level * 16 : level * 16 + 16, member * rows : (member + 1) * rows]
 
 
 def target_kernel(mass_ref, ws_ref, out_ref, lines_ref, *, devices, rows, heads):
@@ -217,17 +262,23 @@
     vmem = pl.BlockSpec(memory_space=pltpu.VMEM)
     params = pltpu.CompilerParams(vmem_limit_bytes=32 * 1024 * 1024)
 
-    query_lines, starts, most = pl.pallas_call(
-        functools.partial(prepare_kernel, scale=scale, rows=rows),
+    query_lines, starts, places, order, most = pl.pallas_call(
+        functools.partial(prepare_kernel, scale=scale, rows=rows, heads=heads),
         out_shape=(
             jax.ShapeDtypeStruct((2 * width, total_rows), jnp.bfloat16),
-            jax.ShapeDtypeStruct((devices, rows), jnp.int32),
+            jax.ShapeDtypeStruct((members, rows), jnp.int32),
+            jax.ShapeDtypeStruct((members, rows), jnp.int32),
+            jax.ShapeDtypeStruct((members * rows, members * rows), jnp.bfloat16),
             jax.ShapeDtypeStruct((8, rows), jnp.float32),
         ),
         in_specs=[vmem] * devices,
-        out_specs=(vmem, vmem, vmem),
+        out_specs=(vmem,) * 5,
+        scratch_shapes=[
+            pltpu.VMEM((devices, width, heads_here * rows), jnp.bfloat16),
+            pltpu.VMEM((devices, 16, rows), jnp.bfloat16),
+        ],
         compiler_params=params,
-        cost_estimate=pl.CostEstimate(flops=10 * width * total_rows, bytes_accessed=2 * 1024 * 1024, transcendentals=0),
+        cost_estimate=pl.CostEstimate(flops=20 * width * total_rows, bytes_accessed=2 * 1024 * 1024, transcendentals=0),
         name="prepare",
     )(*all_queries)
 
@@ -242,7 +293,7 @@
                 score_kernel, members=members, heads=heads, rows=rows, scale=scale, swap=len(earlier)
             ),
             out_shape=(jax.ShapeDtypeStruct((blocks, total_rows), jnp.float32), stat_shape) + (stat_shape,) * len(earlier),
-            in_specs=[vmem] * (4 + len(earlier)),
+            in_specs=[vmem] * (5 + len(earlier)),
             out_specs=(vmem,) * (2 + len(earlier)),
             scratch_shapes=[
                 pltpu.VMEM((members, CHUNK * BLOCK, rows), jnp.float32),
@@ -256,7 +307,7 @@
                 transcendentals=blocks * BLOCK * total_rows,
             ),
             name="score",
-        )(most, starts, query_lines, half_keys, *earlier)
+        )(most, starts, places, query_lines, half_keys, *earlier)
 
     own_sums, own_stat = score(own_keys)
     other_sums, other_stat, stat = score(other_keys, own_stat)
@@ -264,11 +315,11 @@
     mass = pl.pallas_call(
         functools.partial(mass_kernel, members=members, heads=heads, rows=rows),
         out_shape=jax.ShapeDtypeStruct((members, blocks // 16, 2, 16, rows), jnp.float32),
-        in_specs=[vmem] * 5,
+        in_specs=[vmem] * 6,
         out_specs=vmem,
         compiler_params=params,
         name="mass",
-    )(own_sums, other_sums, own_stat, other_stat, stats)
+    )(own_sums, other_sums, own_stat, other_stat, stats, order)
     mass = mass.reshape(devices, blocks // 32, 2, 16, rows)
     mass = lax.all_to_all(mass, GROUP, 0, 0, tiled=True)
     return pl.pallas_call(

time: 121 us -> 115 us (0.950)
  Pallas kernels: 54.6 us -> 49.2 us
    pallas_call x2, Pallas kernels: 53.4 us -> 47.4 us  [score(): pl.pallas_call(functools.partial(score_kernel, members=members, heads=hea...]
  transfers between devices with their start and end apart: 6 -> 6, of which waited for: 3 -> 3; matrix products, arithmetic and copies ran while one was open for 0% -> 0% of each run, Pallas kernels for 22% -> 21%
where the time goes in v6:
time: 115 us; the launch traced here: 114 us
  Pallas kernels  49.2 us (43%)
  starting transfers between devices  31.7 us (28%)
  waiting for transfers between devices  14.8 us (13%)
  blocking collectives  14.8 us (13%)
  local copies, waits for them, and re-layouts  3.57 us (3%)
    pallas_call x2, Pallas kernels, score(): pl.pallas_call(functools.partial(score_kernel, members=members, heads=hea...  47.4 us
    all_to_all x2, starting transfers between devices, spread(): return lax.all_to_all(copies, axes, 0, 0, tiled=True)  19.9 us
    all_to_all x2, waiting for transfers between devices, spread(): return lax.all_to_all(copies, axes, 0, 0, tiled=True)  10.7 us
    ppermute x3, starting transfers between devices, trade(): return lax.ppermute(x, GROUP, [(i, i ^ step) for i in range(devices)])  9.93 us
    all_to_all x1, blocking collectives, body(): mass = lax.all_to_all(mass, GROUP, 0, 0, tiled=True)  7.58 us
    all_to_all x1, blocking collectives, spread(): return lax.all_to_all(copies, axes, 0, 0, tiled=True)  7.18 us
    ppermute x3, waiting for transfers between devices, trade(): return lax.ppermute(x, GROUP, [(i, i ^ step) for i in range(devices)])  4.03 us
  transfers between devices with their start and end apart: 6, of which 3 were waited for; matrix products, arithmetic and copies ran while one was open for 0% of the time, Pallas kernels for 21%

profile of v6, /device:TPU:56, one launch (start us, length us, event | category | flops | bytes accessed | tf_op | source)
XLA Modules:
  0.0 114.2 jit_solution(12925378032380179052)
XLA Ops:
  0.0 0.8 copy-done
  0.8 0.8 broadcast_in_dim.6
  1.5 15.6 %all-to-all-start = ((bf16[16,64,128]{2,1,0:T(8,128)(2,1)}), bf16[16,64,128]{2,1,0:T(8,128)(2,1)S(1)}, u32[]{:S(2)}, u32[]{:S(2)}) async-start(bf16[16,64,128]{2,1,0:T(8,128)(2,1)} %broadcast_in_dim.6), calls=%async_computation | async-start | bytes 524288 | tf_op jit(solution)/shard_map/all_to_all | solution.py:237
  17.1 0.1 copy.4
  17.3 0.0 copy-start.1
  17.3 0.6 copy-done.1
  18.0 10.7 %all-to-all-done = bf16[16,64,128]{2,1,0:T(8,128)(2,1)S(1)} async-done(((bf16[16,64,128]{2,1,0:T(8,128)(2,1)}), bf16[16,64,128]{2,1,0:T(8,128)(2,1)S(1)}, u32[]{:S(2)}, u32[]{:S(2)}) %all-to-all-start) | async-done | bytes 262176 | tf_op jit(solution)/shard_map/all_to_all | solution.py:237
  28.7 1.2 %broadcast_in_dim.7 = bf16[4,16,64,128]{3,2,1,0:T(8,128)(2,1)} broadcast(bf16[16,64,128]{2,1,0:T(8,128)(2,1)S(1)} %all-to-all-done), dimensions={1,2,3} | broadcast | bytes 1310720 | tf_op jit(solution)/shard_map/broadcast_in_dim | solution.py:236
  29.9 4.3 %all-to-all-start.1 = ((bf16[4,16,64,128]{3,2,1,0:T(8,128)(2,1)}), bf16[4,16,64,128]{3,2,1,0:T(8,128)(2,1)S(1)}, u32[]{:S(2)}, u32[]{:S(2)}) async-start(bf16[4,16,64,128]{3,2,1,0:T(8,128)(2,1)} %broadcast_in_dim.7), calls=%async_computation.1 | async-start | bytes 2097152 | tf_op jit(solution)/shard_map/all_to_all | solution.py:237
  34.2 5.0 %collective-permute-start.2 = (bf16[144,512]{1,0:T(8,128)(2,1)S(1)}, bf16[144,512]{1,0:T(8,128)(2,1)S(1)}, u32[]{:S(2)}, u32[]{:S(2)}) collective-permute-start(bf16[144,512]{1,0:T(8,128)(2,1)S(1)} %pad_maximum_fusion.refs_0_), channel_id=1, source_target_pairs={{0,65},{1,64},{64,1},{65,0},{2,67},{3,66},{66,3},{67,2},{4,69},{5,... | collective-permute-start | bytes 442376 | tf_op jit(solution)/shard_map/ppermute | solution.py:254
  39.3 1.9 %collective-permute-start.1 = (bf16[144,512]{1,0:T(8,128)(2,1)S(1)}, bf16[144,512]{1,0:T(8,128)(2,1)S(1)}, u32[]{:S(2)}, u32[]{:S(2)}) collective-permute-start(bf16[144,512]{1,0:T(8,128)(2,1)S(1)} %pad_maximum_fusion.refs_0_), channel_id=1, source_target_pairs={{0,64},{1,65},{64,0},{65,1},{2,66},{3,67},{66,2},{67,3},{4,68},{5,... | collective-permute-start | bytes 442376 | tf_op jit(solution)/shard_map/ppermute | solution.py:254
  41.2 3.0 %collective-permute-start = (bf16[144,512]{1,0:T(8,128)(2,1)S(1)}, bf16[144,512]{1,0:T(8,128)(2,1)S(1)}, u32[]{:S(2)}, u32[]{:S(2)}) collective-permute-start(bf16[144,512]{1,0:T(8,128)(2,1)S(1)} %pad_maximum_fusion.refs_0_), channel_id=1, source_target_pairs={{0,1},{1,0},{64,65},{65,64},{2,3},{3,2},{66,67},{67,66},{4,5},{5,4... | collective-permute-start | bytes 442376 | tf_op jit(solution)/shard_map/ppermute | solution.py:254
  44.2 0.0 collective-permute-done.2.refs_3_
  44.2 2.1 %collective-permute-done.1.refs_2_ = bf16[144,512]{1,0:T(8,128)(2,1)S(1)} collective-permute-done((bf16[144,512]{1,0:T(8,128)(2,1)S(1)}, bf16[144,512]{1,0:T(8,128)(2,1)S(1)}, u32[]{:S(2)}, u32[]{:S(2)}) %collective-permute-start.1) | collective-permute-done | bytes 147488 | tf_op jit(solution)/shard_map/ppermute | solution.py:254
  46.3 1.9 %collective-permute-done.refs_1_ = bf16[144,512]{1,0:T(8,128)(2,1)S(1)} collective-permute-done((bf16[144,512]{1,0:T(8,128)(2,1)S(1)}, bf16[144,512]{1,0:T(8,128)(2,1)S(1)}, u32[]{:S(2)}, u32[]{:S(2)}) %collective-permute-start) | collective-permute-done | bytes 147488 | tf_op jit(solution)/shard_map/ppermute | solution.py:254
  48.2 0.7 prepare.1
  49.0 0.0 all-to-all-done.1.keys_ref
  49.0 1.9 %collective-permute-start.3 = (bf16[4,16,64,128]{3,2,1,0:T(8,128)(2,1)S(1)}, bf16[4,16,64,128]{3,2,1,0:T(8,128)(2,1)S(1)}, u32[]{:S(2)}, u32[]{:S(2)}) collective-permute-start(bf16[4,16,64,128]{3,2,1,0:T(8,128)(2,1)S(1)} %all-to-all-done.1.keys_ref), channel_id=1, source_target_pairs={{0,2},{2,0},{1,3},{3,1},{4,6},{6,4},{5,7},{7,5},{8,10},{10,8},{9,1... | collective-permute-start | bytes 3145736 | tf_op jit(solution)/shard_map/ppermute | solution.py:286
  50.9 23.7 %score.2 = (f32[64,2048]{1,0:T(8,128)S(1)}, f32[2,2048]{1,0:T(2,128)S(1)}) custom-call(f32[8,128]{1,0:T(8,128)S(1)} %get-tuple-element.20.most_ref, s32[2,128]{1,0:T(2,128)S(1)} %get-tuple-element.21.starts_ref, s32[2,128]{1,0:T(2,128)S(1)} %get-tuple-element.22.places_ref, bf16[256,2048]{1,0:T(8,128)(2,1)S(1)} %get-tuple-element.25.lines_ref, ...), custom_call_target="tpu_custom_call" | custom-call | flops 2147483648 | bytes 8388608 | tf_op jit(solution)/shard_map/score/pallas_call | solution.py:291
  74.6 23.7 %score.3 = (f32[64,2048]{1,0:T(8,128)S(1)}, f32[2,2048]{1,0:T(2,128)S(1)}, f32[2,2048]{1,0:T(2,128)S(1)}) custom-call(f32[8,128]{1,0:T(8,128)S(1)} %get-tuple-element.20.most_ref, s32[2,128]{1,0:T(2,128)S(1)} %get-tuple-element.21.starts_ref, s32[2,128]{1,0:T(2,128)S(1)} %get-tuple-element.22.places_ref, bf16[256,2048]{1,0:T(8,128)(2,1)S(1)} %get-tuple-element.25.lines_ref, ...), custom_call_target="tpu_custom_call" | custom-call | flops 2147483648 | bytes 8388608 | tf_op jit(solution)/shard_map/score/pallas_call | solution.py:291
  98.3 7.2 %all_to_all.20.stat_ref = f32[4,2,2048]{2,1,0:T(2,128)S(1)} all-to-all(f32[4,2,2048]{2,1,0:T(2,128)S(1)} %broadcast_in_dim.8), channel_id=1, replica_groups=mesh['yh'=4,'yl'=2,'zh'=4,'x'=4,'core'=2,'head'=2] {'yl','head'}, dimensions={0} | all-to-all | bytes 131072 | tf_op jit(solution)/shard_map/all_to_all | solution.py:237
  105.5 0.3 mass.1
  105.8 7.6 %all_to_all.21.mass_ref = f32[4,2,2,16,128]{4,3,2,1,0:T(8,128)S(1)} all-to-all(f32[4,2,2,16,128]{4,3,2,1,0:T(8,128)S(1)} %bitcast.11), channel_id=1, replica_groups=mesh['yh'=4,'yl'=2,'zh'=4,'x'=4,'core'=2,'head'=2] {'yl','head'}, dimensions={0} | all-to-all | bytes 262144 | tf_op jit(solution)/shard_map/all_to_all | solution.py:324
  113.4 0.8 target.1
  (10 shorter events, 0.1 us)
Async XLA Ops:
  0.0 0.8 copy-start
  1.5 15.6 %copy-start.2 = (bf16[128,4,128]{2,1,0:T(4,128)(2,1)S(1)}, bf16[128,4,128]{2,1,0:T(4,128)(2,1)}, u32[]{:S(2)}) copy-start(bf16[128,4,128]{2,1,0:T(4,128)(2,1)} %param.3) | copy-start | bytes 393220
  1.5 27.2 %all-to-all-start = ((bf16[16,64,128]{2,1,0:T(8,128)(2,1)}), bf16[16,64,128]{2,1,0:T(8,128)(2,1)S(1)}, u32[]{:S(2)}, u32[]{:S(2)}) async-start(bf16[16,64,128]{2,1,0:T(8,128)(2,1)} %broadcast_in_dim.6), calls=%async_computation | async-start | bytes 524288 | tf_op jit(solution)/shard_map/all_to_all | solution.py:237
  17.3 0.7 copy-start.1
  29.9 19.0 %all-to-all-start.1 = ((bf16[4,16,64,128]{3,2,1,0:T(8,128)(2,1)}), bf16[4,16,64,128]{3,2,1,0:T(8,128)(2,1)S(1)}, u32[]{:S(2)}, u32[]{:S(2)}) async-start(bf16[4,16,64,128]{3,2,1,0:T(8,128)(2,1)} %broadcast_in_dim.7), calls=%async_computation.1 | async-start | bytes 2097152 | tf_op jit(solution)/shard_map/all_to_all | solution.py:237
  34.2 10.0 %collective-permute-start.2 = (bf16[144,512]{1,0:T(8,128)(2,1)S(1)}, bf16[144,512]{1,0:T(8,128)(2,1)S(1)}, u32[]{:S(2)}, u32[]{:S(2)}) collective-permute-start(bf16[144,512]{1,0:T(8,128)(2,1)S(1)} %pad_maximum_fusion.refs_0_), channel_id=1, source_target_pairs={{0,65},{1,64},{64,1},{65,0},{2,67},{3,66},{66,3},{67,2},{4,69},{5,... | collective-permute-start | bytes 442376 | tf_op jit(solution)/shard_map/ppermute | solution.py:254
  39.3 7.0 %collective-permute-start.1 = (bf16[144,512]{1,0:T(8,128)(2,1)S(1)}, bf16[144,512]{1,0:T(8,128)(2,1)S(1)}, u32[]{:S(2)}, u32[]{:S(2)}) collective-permute-start(bf16[144,512]{1,0:T(8,128)(2,1)S(1)} %pad_maximum_fusion.refs_0_), channel_id=1, source_target_pairs={{0,64},{1,65},{64,0},{65,1},{2,66},{3,67},{66,2},{67,3},{4,68},{5,... | collective-permute-start | bytes 442376 | tf_op jit(solution)/shard_map/ppermute | solution.py:254
  41.2 7.0 %collective-permute-start = (bf16[144,512]{1,0:T(8,128)(2,1)S(1)}, bf16[144,512]{1,0:T(8,128)(2,1)S(1)}, u32[]{:S(2)}, u32[]{:S(2)}) collective-permute-start(bf16[144,512]{1,0:T(8,128)(2,1)S(1)} %pad_maximum_fusion.refs_0_), channel_id=1, source_target_pairs={{0,1},{1,0},{64,65},{65,64},{2,3},{3,2},{66,67},{67,66},{4,5},{5,4... | collective-permute-start | bytes 442376 | tf_op jit(solution)/shard_map/ppermute | solution.py:254
  49.0 25.6 %collective-permute-start.3 = (bf16[4,16,64,128]{3,2,1,0:T(8,128)(2,1)S(1)}, bf16[4,16,64,128]{3,2,1,0:T(8,128)(2,1)S(1)}, u32[]{:S(2)}, u32[]{:S(2)}) collective-permute-start(bf16[4,16,64,128]{3,2,1,0:T(8,128)(2,1)S(1)} %all-to-all-done.1.keys_ref), channel_id=1, source_target_pairs={{0,2},{2,0},{1,3},{3,1},{4,6},{6,4},{5,7},{7,5},{8,10},{10,8},{9,1... | collective-permute-start | bytes 3145736 | tf_op jit(solution)/shard_map/ppermute | solution.py:286

commit v7 on v5

--- a/solution.py
+++ b/solution.py
@@ -209,9 +209,10 @@
         return lax.ppermute(x, GROUP, [(i, i ^ step) for i in range(devices)])
 
     own = lax.dynamic_slice_in_dim(keys, lax.axis_index("head") * BLOCK, BLOCK, 0)
-    column, lines = lax.optimization_barrier((spread(own, ("yh", "zh")), lines))
+    column, lines, near = lax.optimization_barrier((spread(own, ("yh", "zh")), lines, trade(lines, 1)))
     own_keys = spread(column, "x")
-    all_queries = [lines, trade(lines, 1), trade(lines, 2), trade(lines, 3)]
+    across, along = trade(lines, 3), trade(lines, 2)
+    all_queries = [lines, near, along, across]
 
     total_rows = members * heads * rows
     vmem = pl.BlockSpec(memory_space=pltpu.VMEM)

time: 121 us -> 121 us (level)
    ppermute x3, waiting for transfers between devices: 4.03 us -> 12.6 us  [trade(): return lax.ppermute(x, GROUP, [(i, i ^ step) for i in range(devices)])]
    all_to_all x2, waiting for transfers between devices: 10.7 us -> 2.46 us  [spread(): return lax.all_to_all(copies, axes, 0, 0, tiled=True)]
  transfers between devices with their start and end apart: 6 -> 6, of which waited for: 3 -> 5; matrix products, arithmetic and copies ran while one was open for 0% -> 0% of each run, Pallas kernels for 22% -> 22%
where the time goes in v7:
time: 121 us; the launch traced here: 120 us
  Pallas kernels  54.7 us (45%)
  starting transfers between devices  32.1 us (27%)
  waiting for transfers between devices  15.1 us (12%)
  blocking collectives  14.9 us (12%)
  local copies, waits for them, and re-layouts  3.57 us (3%)
    pallas_call x2, Pallas kernels, score(): pl.pallas_call(functools.partial(score_kernel, members=members, heads=hea...  53.4 us
    all_to_all x2, starting transfers between devices, spread(): return lax.all_to_all(copies, axes, 0, 0, tiled=True)  19.9 us
    ppermute x3, waiting for transfers between devices, trade(): return lax.ppermute(x, GROUP, [(i, i ^ step) for i in range(devices)])  12.6 us
    ppermute x3, starting transfers between devices, trade(): return lax.ppermute(x, GROUP, [(i, i ^ step) for i in range(devices)])  10.3 us
    all_to_all x1, blocking collectives, body(): mass = lax.all_to_all(mass, GROUP, 0, 0, tiled=True)  7.58 us
    all_to_all x1, blocking collectives, spread(): return lax.all_to_all(copies, axes, 0, 0, tiled=True)  7.35 us
    all_to_all x2, waiting for transfers between devices, spread(): return lax.all_to_all(copies, axes, 0, 0, tiled=True)  2.46 us
  transfers between devices with their start and end apart: 6, of which 5 were waited for; matrix products, arithmetic and copies ran while one was open for 0% of the time, Pallas kernels for 22%

profile of v7, /device:TPU:56, one launch (start us, length us, event | category | flops | bytes accessed | tf_op | source)
XLA Modules:
  0.0 120.5 jit_solution(5376282724818442183)
XLA Ops:
  0.0 0.8 copy-done
  0.8 0.8 broadcast_in_dim.6
  1.5 15.6 %all-to-all-start = ((bf16[16,64,128]{2,1,0:T(8,128)(2,1)}), bf16[16,64,128]{2,1,0:T(8,128)(2,1)S(1)}, u32[]{:S(2)}, u32[]{:S(2)}) async-start(bf16[16,64,128]{2,1,0:T(8,128)(2,1)} %broadcast_in_dim.6), calls=%async_computation | async-start | bytes 524288 | tf_op jit(solution)/shard_map/all_to_all | solution.py:192
  17.1 0.1 copy.4
  17.3 0.0 copy-start.1
  17.3 0.6 copy-done.1
  18.0 3.4 %collective-permute-start = (bf16[144,512]{1,0:T(8,128)(2,1)S(1)}, bf16[144,512]{1,0:T(8,128)(2,1)S(1)}, u32[]{:S(2)}, u32[]{:S(2)}) collective-permute-start(bf16[144,512]{1,0:T(8,128)(2,1)S(1)} %pad_maximum_fusion.refs_0_), channel_id=1, source_target_pairs={{0,1},{1,0},{64,65},{65,64},{2,3},{3,2},{66,67},{67,66},{4,5},{5,4... | collective-permute-start | bytes 442376 | tf_op jit(solution)/shard_map/ppermute | solution.py:209
  21.4 7.0 %collective-permute-done.refs_1_ = bf16[144,512]{1,0:T(8,128)(2,1)S(1)} collective-permute-done((bf16[144,512]{1,0:T(8,128)(2,1)S(1)}, bf16[144,512]{1,0:T(8,128)(2,1)S(1)}, u32[]{:S(2)}, u32[]{:S(2)}) %collective-permute-start) | collective-permute-done | bytes 147488 | tf_op jit(solution)/shard_map/ppermute | solution.py:209
  28.4 0.4 all-to-all-done
  28.7 1.2 %broadcast_in_dim.7 = bf16[4,16,64,128]{3,2,1,0:T(8,128)(2,1)} broadcast(bf16[16,64,128]{2,1,0:T(8,128)(2,1)S(1)} %all-to-all-done), dimensions={1,2,3} | broadcast | bytes 1310720 | tf_op jit(solution)/shard_map/broadcast_in_dim | solution.py:191
  30.0 4.3 %all-to-all-start.1 = ((bf16[4,16,64,128]{3,2,1,0:T(8,128)(2,1)}), bf16[4,16,64,128]{3,2,1,0:T(8,128)(2,1)S(1)}, u32[]{:S(2)}, u32[]{:S(2)}) async-start(bf16[4,16,64,128]{3,2,1,0:T(8,128)(2,1)} %broadcast_in_dim.7), calls=%async_computation.1 | async-start | bytes 2097152 | tf_op jit(solution)/shard_map/all_to_all | solution.py:192
  34.3 4.6 %collective-permute-start.1 = (bf16[144,512]{1,0:T(8,128)(2,1)S(1)}, bf16[144,512]{1,0:T(8,128)(2,1)S(1)}, u32[]{:S(2)}, u32[]{:S(2)}) collective-permute-start(bf16[144,512]{1,0:T(8,128)(2,1)S(1)} %pad_maximum_fusion.refs_0_), channel_id=1, source_target_pairs={{0,64},{1,65},{64,0},{65,1},{2,66},{3,67},{66,2},{67,3},{4,68},{5,... | collective-permute-start | bytes 442376 | tf_op jit(solution)/shard_map/ppermute | solution.py:209
  38.9 2.3 %collective-permute-start.2 = (bf16[144,512]{1,0:T(8,128)(2,1)S(1)}, bf16[144,512]{1,0:T(8,128)(2,1)S(1)}, u32[]{:S(2)}, u32[]{:S(2)}) collective-permute-start(bf16[144,512]{1,0:T(8,128)(2,1)S(1)} %pad_maximum_fusion.refs_0_), channel_id=1, source_target_pairs={{0,65},{1,64},{64,1},{65,0},{2,67},{3,66},{66,3},{67,2},{4,69},{5,... | collective-permute-start | bytes 442376 | tf_op jit(solution)/shard_map/ppermute | solution.py:209
  41.2 1.6 %collective-permute-done.1.refs_2_ = bf16[144,512]{1,0:T(8,128)(2,1)S(1)} collective-permute-done((bf16[144,512]{1,0:T(8,128)(2,1)S(1)}, bf16[144,512]{1,0:T(8,128)(2,1)S(1)}, u32[]{:S(2)}, u32[]{:S(2)}) %collective-permute-start.1) | collective-permute-done | bytes 147488 | tf_op jit(solution)/shard_map/ppermute | solution.py:209
  42.8 4.0 %collective-permute-done.2.refs_3_ = bf16[144,512]{1,0:T(8,128)(2,1)S(1)} collective-permute-done((bf16[144,512]{1,0:T(8,128)(2,1)S(1)}, bf16[144,512]{1,0:T(8,128)(2,1)S(1)}, u32[]{:S(2)}, u32[]{:S(2)}) %collective-permute-start.2) | collective-permute-done | bytes 147488 | tf_op jit(solution)/shard_map/ppermute | solution.py:209
  46.8 0.4 prepare.1
  47.2 2.1 %all-to-all-done.1.keys_ref = bf16[4,16,64,128]{3,2,1,0:T(8,128)(2,1)S(1)} async-done(((bf16[4,16,64,128]{3,2,1,0:T(8,128)(2,1)}), bf16[4,16,64,128]{3,2,1,0:T(8,128)(2,1)S(1)}, u32[]{:S(2)}, u32[]{:S(2)}) %all-to-all-start.1) | async-done | bytes 1048608 | tf_op jit(solution)/shard_map/all_to_all | solution.py:192
  49.3 1.9 %collective-permute-start.3 = (bf16[4,16,64,128]{3,2,1,0:T(8,128)(2,1)S(1)}, bf16[4,16,64,128]{3,2,1,0:T(8,128)(2,1)S(1)}, u32[]{:S(2)}, u32[]{:S(2)}) collective-permute-start(bf16[4,16,64,128]{3,2,1,0:T(8,128)(2,1)S(1)} %all-to-all-done.1.keys_ref), channel_id=1, source_target_pairs={{0,2},{2,0},{1,3},{3,1},{4,6},{6,4},{5,7},{7,5},{8,10},{10,8},{9,1... | collective-permute-start | bytes 3145736 | tf_op jit(solution)/shard_map/ppermute | solution.py:236
  51.2 26.7 %score.2 = (f32[64,2048]{1,0:T(8,128)S(1)}, f32[2,2048]{1,0:T(2,128)S(1)}) custom-call(f32[8,128]{1,0:T(8,128)S(1)} %get-tuple-element.20.most_ref, s32[4,128]{1,0:T(4,128)S(1)} %get-tuple-element.21.starts_ref, bf16[256,2048]{1,0:T(8,128)(2,1)S(1)} %get-tuple-element.24.lines_ref, bf16[4,16,64,128]{3,2,1,0:T(8,128)(2,1)S(1)} %all-to-all-done.1.keys_ref), custom_call_target="tpu_custom_call" | custom-call | flops 2147483648 | bytes 8388608 | tf_op jit(solution)/shard_map/score/pallas_call | solution.py:241
  77.9 26.7 %score.3 = (f32[64,2048]{1,0:T(8,128)S(1)}, f32[2,2048]{1,0:T(2,128)S(1)}, f32[2,2048]{1,0:T(2,128)S(1)}) custom-call(f32[8,128]{1,0:T(8,128)S(1)} %get-tuple-element.20.most_ref, s32[4,128]{1,0:T(4,128)S(1)} %get-tuple-element.21.starts_ref, bf16[256,2048]{1,0:T(8,128)(2,1)S(1)} %get-tuple-element.24.lines_ref, ...), custom_call_target="tpu_custom_call" | custom-call | flops 2147483648 | bytes 8388608 | tf_op jit(solution)/shard_map/score/pallas_call | solution.py:241
  104.6 7.3 %all_to_all.20.stat_ref = f32[4,2,2048]{2,1,0:T(2,128)S(1)} all-to-all(f32[4,2,2048]{2,1,0:T(2,128)S(1)} %broadcast_in_dim.8), channel_id=1, replica_groups=mesh['yh'=4,'yl'=2,'zh'=4,'x'=4,'core'=2,'head'=2] {'yl','head'}, dimensions={0} | all-to-all | bytes 131072 | tf_op jit(solution)/shard_map/all_to_all | solution.py:192
  112.0 0.1 mass.1
  112.1 7.6 %all_to_all.21.mass_ref = f32[4,2,2,16,128]{4,3,2,1,0:T(8,128)S(1)} all-to-all(f32[4,2,2,16,128]{4,3,2,1,0:T(8,128)S(1)} %bitcast.11), channel_id=1, replica_groups=mesh['yh'=4,'yl'=2,'zh'=4,'x'=4,'core'=2,'head'=2] {'yl','head'}, dimensions={0} | all-to-all | bytes 262144 | tf_op jit(solution)/shard_map/all_to_all | solution.py:274
  119.7 0.8 target.1
  (10 shorter events, 0.1 us)
Async XLA Ops:
  0.0 0.8 copy-start
  1.5 15.6 %copy-start.2 = (bf16[128,4,128]{2,1,0:T(4,128)(2,1)S(1)}, bf16[128,4,128]{2,1,0:T(4,128)(2,1)}, u32[]{:S(2)}) copy-start(bf16[128,4,128]{2,1,0:T(4,128)(2,1)} %param.3) | copy-start | bytes 393220
  1.5 27.2 %all-to-all-start = ((bf16[16,64,128]{2,1,0:T(8,128)(2,1)}), bf16[16,64,128]{2,1,0:T(8,128)(2,1)S(1)}, u32[]{:S(2)}, u32[]{:S(2)}) async-start(bf16[16,64,128]{2,1,0:T(8,128)(2,1)} %broadcast_in_dim.6), calls=%async_computation | async-start | bytes 524288 | tf_op jit(solution)/shard_map/all_to_all | solution.py:192
  17.3 0.7 copy-start.1
  18.0 10.4 %collective-permute-start = (bf16[144,512]{1,0:T(8,128)(2,1)S(1)}, bf16[144,512]{1,0:T(8,128)(2,1)S(1)}, u32[]{:S(2)}, u32[]{:S(2)}) collective-permute-start(bf16[144,512]{1,0:T(8,128)(2,1)S(1)} %pad_maximum_fusion.refs_0_), channel_id=1, source_target_pairs={{0,1},{1,0},{64,65},{65,64},{2,3},{3,2},{66,67},{67,66},{4,5},{5,4... | collective-permute-start | bytes 442376 | tf_op jit(solution)/shard_map/ppermute | solution.py:209
  30.0 19.3 %all-to-all-start.1 = ((bf16[4,16,64,128]{3,2,1,0:T(8,128)(2,1)}), bf16[4,16,64,128]{3,2,1,0:T(8,128)(2,1)S(1)}, u32[]{:S(2)}, u32[]{:S(2)}) async-start(bf16[4,16,64,128]{3,2,1,0:T(8,128)(2,1)} %broadcast_in_dim.7), calls=%async_computation.1 | async-start | bytes 2097152 | tf_op jit(solution)/shard_map/all_to_all | solution.py:192
  34.3 8.6 %collective-permute-start.1 = (bf16[144,512]{1,0:T(8,128)(2,1)S(1)}, bf16[144,512]{1,0:T(8,128)(2,1)S(1)}, u32[]{:S(2)}, u32[]{:S(2)}) collective-permute-start(bf16[144,512]{1,0:T(8,128)(2,1)S(1)} %pad_maximum_fusion.refs_0_), channel_id=1, source_target_pairs={{0,64},{1,65},{64,0},{65,1},{2,66},{3,67},{66,2},{67,3},{4,68},{5,... | collective-permute-start | bytes 442376 | tf_op jit(solution)/shard_map/ppermute | solution.py:209
  38.9 7.9 %collective-permute-start.2 = (bf16[144,512]{1,0:T(8,128)(2,1)S(1)}, bf16[144,512]{1,0:T(8,128)(2,1)S(1)}, u32[]{:S(2)}, u32[]{:S(2)}) collective-permute-start(bf16[144,512]{1,0:T(8,128)(2,1)S(1)} %pad_maximum_fusion.refs_0_), channel_id=1, source_target_pairs={{0,65},{1,64},{64,1},{65,0},{2,67},{3,66},{66,3},{67,2},{4,69},{5,... | collective-permute-start | bytes 442376 | tf_op jit(solution)/shard_map/ppermute | solution.py:209
  49.3 28.6 %collective-permute-start.3 = (bf16[4,16,64,128]{3,2,1,0:T(8,128)(2,1)S(1)}, bf16[4,16,64,128]{3,2,1,0:T(8,128)(2,1)S(1)}, u32[]{:S(2)}, u32[]{:S(2)}) collective-permute-start(bf16[4,16,64,128]{3,2,1,0:T(8,128)(2,1)S(1)} %all-to-all-done.1.keys_ref), channel_id=1, source_target_pairs={{0,2},{2,0},{1,3},{3,1},{4,6},{6,4},{5,7},{7,5},{8,10},{10,8},{9,1... | collective-permute-start | bytes 3145736 | tf_op jit(solution)/shard_map/ppermute | solution.py:236

commit v8 on v7

--- a/solution.py
+++ b/solution.py
@@ -80,11 +80,13 @@
         shard_of(group, member, core) * rows + lax.broadcasted_iota(jnp.int32, (1, rows), 1) for member in range(members)
     ]
 
-    def fill_mask(chunk, inside, outside):
+    def fill_mask(chunk, causal, inside, outside):
         for block in range(CHUNK):
             base = (shard_of(chunk * CHUNK + block, mine // 2, side) * 2 + mine % 2) * BLOCK
             for member in range(members):
-                allowed = (line >= starts[member] - base) & (line <= places[member] - base)
+                allowed = line >= starts[member] - base
+                if causal:
+                    allowed = allowed & (line <= places[member] - base)
                 mask_ref[member, block * BLOCK : (block + 1) * BLOCK, :] = jnp.where(allowed, inside, outside)
 
     def scores(keys, at):
@@ -95,9 +97,9 @@
 
     @pl.when(safe)
     def _():
-        def one_chunk(chunk, carry):
+        def one_chunk(chunk, carry, causal=False):
             keys = chunk_keys(chunk)
-            fill_mask(chunk, 1.0, 0.0)
+            fill_mask(chunk, causal, 1.0, 0.0)
             for tile in range(members * width // pair):
                 at = tile * pair
                 result = scores(keys, at)
@@ -117,11 +119,12 @@
                     sums_ref[lines_of(chunk), at + column * rows : at + (column + 1) * rows] = total
             return carry
 
-        lax.fori_loop(first_chunk, last_chunk + 1, one_chunk, 0)
+        lax.fori_loop(first_chunk, last_chunk, one_chunk, 0)
+        one_chunk(last_chunk, 0, causal=True)
 
     def each_tile(visit):
         def one_chunk(chunk, carry):
-            fill_mask(chunk, 0.0, LOW)
+            fill_mask(chunk, True, 0.0, LOW)
 
             def one_tile(tile, carry):
                 at = pl.multiple_of(tile * pair, pair)

time: 121 us -> 121 us (level)
  no operation moved by 1% of the time
where the time goes in v8:
time: 121 us; the launch traced here: 120 us
  Pallas kernels  54.6 us (45%)
  starting transfers between devices  32.1 us (27%)
  waiting for transfers between devices  15.1 us (12%)
  blocking collectives  15 us (12%)
  local copies, waits for them, and re-layouts  3.57 us (3%)
    pallas_call x2, Pallas kernels, score(): pl.pallas_call(functools.partial(score_kernel, members=members, heads=hea...  53.3 us
    all_to_all x2, starting transfers between devices, spread(): return lax.all_to_all(copies, axes, 0, 0, tiled=True)  19.9 us
    ppermute x3, waiting for transfers between devices, trade(): return lax.ppermute(x, GROUP, [(i, i ^ step) for i in range(devices)])  12.6 us
    ppermute x3, starting transfers between devices, trade(): return lax.ppermute(x, GROUP, [(i, i ^ step) for i in range(devices)])  10.3 us
    all_to_all x1, blocking collectives, body(): mass = lax.all_to_all(mass, GROUP, 0, 0, tiled=True)  7.58 us
    all_to_all x1, blocking collectives, spread(): return lax.all_to_all(copies, axes, 0, 0, tiled=True)  7.38 us
    all_to_all x2, waiting for transfers between devices, spread(): return lax.all_to_all(copies, axes, 0, 0, tiled=True)  2.46 us
  transfers between devices with their start and end apart: 6, of which 5 were waited for; matrix products, arithmetic and copies ran while one was open for 0% of the time, Pallas kernels for 22%

profile of v8, /device:TPU:56, one launch (start us, length us, event | category | flops | bytes accessed | tf_op | source)
XLA Modules:
  0.0 120.4 jit_solution(5847071469169435317)
XLA Ops:
  0.0 0.8 copy-done
  0.8 0.8 broadcast_in_dim.6
  1.5 15.6 %all-to-all-start = ((bf16[16,64,128]{2,1,0:T(8,128)(2,1)}), bf16[16,64,128]{2,1,0:T(8,128)(2,1)S(1)}, u32[]{:S(2)}, u32[]{:S(2)}) async-start(bf16[16,64,128]{2,1,0:T(8,128)(2,1)} %broadcast_in_dim.6), calls=%async_computation | async-start | bytes 524288 | tf_op jit(solution)/shard_map/all_to_all | solution.py:195
  17.1 0.1 copy.4
  17.3 0.0 copy-start.1
  17.3 0.6 copy-done.1
  18.0 3.4 %collective-permute-start = (bf16[144,512]{1,0:T(8,128)(2,1)S(1)}, bf16[144,512]{1,0:T(8,128)(2,1)S(1)}, u32[]{:S(2)}, u32[]{:S(2)}) collective-permute-start(bf16[144,512]{1,0:T(8,128)(2,1)S(1)} %pad_maximum_fusion.refs_0_), channel_id=1, source_target_pairs={{0,1},{1,0},{64,65},{65,64},{2,3},{3,2},{66,67},{67,66},{4,5},{5,4... | collective-permute-start | bytes 442376 | tf_op jit(solution)/shard_map/ppermute | solution.py:212
  21.4 7.0 %collective-permute-done.refs_1_ = bf16[144,512]{1,0:T(8,128)(2,1)S(1)} collective-permute-done((bf16[144,512]{1,0:T(8,128)(2,1)S(1)}, bf16[144,512]{1,0:T(8,128)(2,1)S(1)}, u32[]{:S(2)}, u32[]{:S(2)}) %collective-permute-start) | collective-permute-done | bytes 147488 | tf_op jit(solution)/shard_map/ppermute | solution.py:212
  28.4 0.4 all-to-all-done
  28.7 1.2 %broadcast_in_dim.7 = bf16[4,16,64,128]{3,2,1,0:T(8,128)(2,1)} broadcast(bf16[16,64,128]{2,1,0:T(8,128)(2,1)S(1)} %all-to-all-done), dimensions={1,2,3} | broadcast | bytes 1310720 | tf_op jit(solution)/shard_map/broadcast_in_dim | solution.py:194
  30.0 4.3 %all-to-all-start.1 = ((bf16[4,16,64,128]{3,2,1,0:T(8,128)(2,1)}), bf16[4,16,64,128]{3,2,1,0:T(8,128)(2,1)S(1)}, u32[]{:S(2)}, u32[]{:S(2)}) async-start(bf16[4,16,64,128]{3,2,1,0:T(8,128)(2,1)} %broadcast_in_dim.7), calls=%async_computation.1 | async-start | bytes 2097152 | tf_op jit(solution)/shard_map/all_to_all | solution.py:195
  34.3 4.6 %collective-permute-start.1 = (bf16[144,512]{1,0:T(8,128)(2,1)S(1)}, bf16[144,512]{1,0:T(8,128)(2,1)S(1)}, u32[]{:S(2)}, u32[]{:S(2)}) collective-permute-start(bf16[144,512]{1,0:T(8,128)(2,1)S(1)} %pad_maximum_fusion.refs_0_), channel_id=1, source_target_pairs={{0,64},{1,65},{64,0},{65,1},{2,66},{3,67},{66,2},{67,3},{4,68},{5,... | collective-permute-start | bytes 442376 | tf_op jit(solution)/shard_map/ppermute | solution.py:212
  38.9 2.3 %collective-permute-start.2 = (bf16[144,512]{1,0:T(8,128)(2,1)S(1)}, bf16[144,512]{1,0:T(8,128)(2,1)S(1)}, u32[]{:S(2)}, u32[]{:S(2)}) collective-permute-start(bf16[144,512]{1,0:T(8,128)(2,1)S(1)} %pad_maximum_fusion.refs_0_), channel_id=1, source_target_pairs={{0,65},{1,64},{64,1},{65,0},{2,67},{3,66},{66,3},{67,2},{4,69},{5,... | collective-permute-start | bytes 442376 | tf_op jit(solution)/shard_map/ppermute | solution.py:212
  41.2 1.6 %collective-permute-done.1.refs_2_ = bf16[144,512]{1,0:T(8,128)(2,1)S(1)} collective-permute-done((bf16[144,512]{1,0:T(8,128)(2,1)S(1)}, bf16[144,512]{1,0:T(8,128)(2,1)S(1)}, u32[]{:S(2)}, u32[]{:S(2)}) %collective-permute-start.1) | collective-permute-done | bytes 147488 | tf_op jit(solution)/shard_map/ppermute | solution.py:212
  42.8 4.0 %collective-permute-done.2.refs_3_ = bf16[144,512]{1,0:T(8,128)(2,1)S(1)} collective-permute-done((bf16[144,512]{1,0:T(8,128)(2,1)S(1)}, bf16[144,512]{1,0:T(8,128)(2,1)S(1)}, u32[]{:S(2)}, u32[]{:S(2)}) %collective-permute-start.2) | collective-permute-done | bytes 147488 | tf_op jit(solution)/shard_map/ppermute | solution.py:212
  46.8 0.4 prepare.1
  47.2 2.1 %all-to-all-done.1.keys_ref = bf16[4,16,64,128]{3,2,1,0:T(8,128)(2,1)S(1)} async-done(((bf16[4,16,64,128]{3,2,1,0:T(8,128)(2,1)}), bf16[4,16,64,128]{3,2,1,0:T(8,128)(2,1)S(1)}, u32[]{:S(2)}, u32[]{:S(2)}) %all-to-all-start.1) | async-done | bytes 1048608 | tf_op jit(solution)/shard_map/all_to_all | solution.py:195
  49.3 1.9 %collective-permute-start.3 = (bf16[4,16,64,128]{3,2,1,0:T(8,128)(2,1)S(1)}, bf16[4,16,64,128]{3,2,1,0:T(8,128)(2,1)S(1)}, u32[]{:S(2)}, u32[]{:S(2)}) collective-permute-start(bf16[4,16,64,128]{3,2,1,0:T(8,128)(2,1)S(1)} %all-to-all-done.1.keys_ref), channel_id=1, source_target_pairs={{0,2},{2,0},{1,3},{3,1},{4,6},{6,4},{5,7},{7,5},{8,10},{10,8},{9,1... | collective-permute-start | bytes 3145736 | tf_op jit(solution)/shard_map/ppermute | solution.py:239
  51.2 26.6 %score.2 = (f32[64,2048]{1,0:T(8,128)S(1)}, f32[2,2048]{1,0:T(2,128)S(1)}) custom-call(f32[8,128]{1,0:T(8,128)S(1)} %get-tuple-element.20.most_ref, s32[4,128]{1,0:T(4,128)S(1)} %get-tuple-element.21.starts_ref, bf16[256,2048]{1,0:T(8,128)(2,1)S(1)} %get-tuple-element.24.lines_ref, bf16[4,16,64,128]{3,2,1,0:T(8,128)(2,1)S(1)} %all-to-all-done.1.keys_ref), custom_call_target="tpu_custom_call" | custom-call | flops 2147483648 | bytes 8388608 | tf_op jit(solution)/shard_map/score/pallas_call | solution.py:244
  77.8 26.7 %score.3 = (f32[64,2048]{1,0:T(8,128)S(1)}, f32[2,2048]{1,0:T(2,128)S(1)}, f32[2,2048]{1,0:T(2,128)S(1)}) custom-call(f32[8,128]{1,0:T(8,128)S(1)} %get-tuple-element.20.most_ref, s32[4,128]{1,0:T(4,128)S(1)} %get-tuple-element.21.starts_ref, bf16[256,2048]{1,0:T(8,128)(2,1)S(1)} %get-tuple-element.24.lines_ref, ...), custom_call_target="tpu_custom_call" | custom-call | flops 2147483648 | bytes 8388608 | tf_op jit(solution)/shard_map/score/pallas_call | solution.py:244
  104.6 7.4 %all_to_all.20.stat_ref = f32[4,2,2048]{2,1,0:T(2,128)S(1)} all-to-all(f32[4,2,2048]{2,1,0:T(2,128)S(1)} %broadcast_in_dim.8), channel_id=1, replica_groups=mesh['yh'=4,'yl'=2,'zh'=4,'x'=4,'core'=2,'head'=2] {'yl','head'}, dimensions={0} | all-to-all | bytes 131072 | tf_op jit(solution)/shard_map/all_to_all | solution.py:195
  111.9 0.1 mass.1
  112.1 7.6 %all_to_all.21.mass_ref = f32[4,2,2,16,128]{4,3,2,1,0:T(8,128)S(1)} all-to-all(f32[4,2,2,16,128]{4,3,2,1,0:T(8,128)S(1)} %bitcast.11), channel_id=1, replica_groups=mesh['yh'=4,'yl'=2,'zh'=4,'x'=4,'core'=2,'head'=2] {'yl','head'}, dimensions={0} | all-to-all | bytes 262144 | tf_op jit(solution)/shard_map/all_to_all | solution.py:277
  119.7 0.8 target.1
  (10 shorter events, 0.1 us)
Async XLA Ops:
  0.0 0.8 copy-start
  1.5 15.6 %copy-start.2 = (bf16[128,4,128]{2,1,0:T(4,128)(2,1)S(1)}, bf16[128,4,128]{2,1,0:T(4,128)(2,1)}, u32[]{:S(2)}) copy-start(bf16[128,4,128]{2,1,0:T(4,128)(2,1)} %param.3) | copy-start | bytes 393220
  1.5 27.2 %all-to-all-start = ((bf16[16,64,128]{2,1,0:T(8,128)(2,1)}), bf16[16,64,128]{2,1,0:T(8,128)(2,1)S(1)}, u32[]{:S(2)}, u32[]{:S(2)}) async-start(bf16[16,64,128]{2,1,0:T(8,128)(2,1)} %broadcast_in_dim.6), calls=%async_computation | async-start | bytes 524288 | tf_op jit(solution)/shard_map/all_to_all | solution.py:195
  17.3 0.7 copy-start.1
  18.0 10.4 %collective-permute-start = (bf16[144,512]{1,0:T(8,128)(2,1)S(1)}, bf16[144,512]{1,0:T(8,128)(2,1)S(1)}, u32[]{:S(2)}, u32[]{:S(2)}) collective-permute-start(bf16[144,512]{1,0:T(8,128)(2,1)S(1)} %pad_maximum_fusion.refs_0_), channel_id=1, source_target_pairs={{0,1},{1,0},{64,65},{65,64},{2,3},{3,2},{66,67},{67,66},{4,5},{5,4... | collective-permute-start | bytes 442376 | tf_op jit(solution)/shard_map/ppermute | solution.py:212
  30.0 19.3 %all-to-all-start.1 = ((bf16[4,16,64,128]{3,2,1,0:T(8,128)(2,1)}), bf16[4,16,64,128]{3,2,1,0:T(8,128)(2,1)S(1)}, u32[]{:S(2)}, u32[]{:S(2)}) async-start(bf16[4,16,64,128]{3,2,1,0:T(8,128)(2,1)} %broadcast_in_dim.7), calls=%async_computation.1 | async-start | bytes 2097152 | tf_op jit(solution)/shard_map/all_to_all | solution.py:195
  34.3 8.6 %collective-permute-start.1 = (bf16[144,512]{1,0:T(8,128)(2,1)S(1)}, bf16[144,512]{1,0:T(8,128)(2,1)S(1)}, u32[]{:S(2)}, u32[]{:S(2)}) collective-permute-start(bf16[144,512]{1,0:T(8,128)(2,1)S(1)} %pad_maximum_fusion.refs_0_), channel_id=1, source_target_pairs={{0,64},{1,65},{64,0},{65,1},{2,66},{3,67},{66,2},{67,3},{4,68},{5,... | collective-permute-start | bytes 442376 | tf_op jit(solution)/shard_map/ppermute | solution.py:212
  38.9 7.9 %collective-permute-start.2 = (bf16[144,512]{1,0:T(8,128)(2,1)S(1)}, bf16[144,512]{1,0:T(8,128)(2,1)S(1)}, u32[]{:S(2)}, u32[]{:S(2)}) collective-permute-start(bf16[144,512]{1,0:T(8,128)(2,1)S(1)} %pad_maximum_fusion.refs_0_), channel_id=1, source_target_pairs={{0,65},{1,64},{64,1},{65,0},{2,67},{3,66},{66,3},{67,2},{4,69},{5,... | collective-permute-start | bytes 442376 | tf_op jit(solution)/shard_map/ppermute | solution.py:212
  49.3 28.6 %collective-permute-start.3 = (bf16[4,16,64,128]{3,2,1,0:T(8,128)(2,1)S(1)}, bf16[4,16,64,128]{3,2,1,0:T(8,128)(2,1)S(1)}, u32[]{:S(2)}, u32[]{:S(2)}) collective-permute-start(bf16[4,16,64,128]{3,2,1,0:T(8,128)(2,1)S(1)} %all-to-all-done.1.keys_ref), channel_id=1, source_target_pairs={{0,2},{2,0},{1,3},{3,1},{4,6},{6,4},{5,7},{7,5},{8,10},{10,8},{9,1... | collective-permute-start | bytes 3145736 | tf_op jit(solution)/shard_map/ppermute | solution.py:239

commit v9 on v8

--- a/solution.py
+++ b/solution.py
@@ -63,7 +63,6 @@
     largest = jnp.max(jnp.abs(keys_ref[...]), axis=1).astype(jnp.float32)
     longest = jnp.max(jnp.sum(largest * largest, axis=-1))
     safe = jnp.max(most_ref[...]) * longest * (scale * scale) <= SAFE * SAFE
-    sums_ref[...] = jnp.zeros_like(sums_ref)
 
     starts = [starts_ref[2 * member : 2 * member + 1, :] for member in range(members)]
     first_start = jnp.min(functools.reduce(jnp.minimum, starts))
@@ -94,6 +93,13 @@
 
     def lines_of(chunk):
         return pl.ds(pl.multiple_of(chunk * CHUNK, CHUNK), CHUNK)
+
+    def clear(chunk, carry):
+        sums_ref[lines_of(chunk), :] = jnp.zeros((CHUNK, sums_ref.shape[1]), jnp.float32)
+        return carry
+
+    lax.fori_loop(0, first_chunk, clear, 0)
+    lax.fori_loop(last_chunk + 1, sums_ref.shape[0] // CHUNK, clear, 0)
 
     @pl.when(safe)
     def _():

time: 121 us -> 121 us (level)
  no operation moved by 1% of the time
where the time goes in v9:
time: 121 us; the launch traced here: 120 us
  Pallas kernels  54.6 us (45%)
  starting transfers between devices  32.1 us (27%)
  waiting for transfers between devices  15.1 us (12%)
  blocking collectives  15 us (12%)
  local copies, waits for them, and re-layouts  3.57 us (3%)
    pallas_call x2, Pallas kernels, score(): pl.pallas_call(functools.partial(score_kernel, members=members, heads=hea...  53.4 us
    all_to_all x2, starting transfers between devices, spread(): return lax.all_to_all(copies, axes, 0, 0, tiled=True)  19.9 us
    ppermute x3, waiting for transfers between devices, trade(): return lax.ppermute(x, GROUP, [(i, i ^ step) for i in range(devices)])  12.6 us
    ppermute x3, starting transfers between devices, trade(): return lax.ppermute(x, GROUP, [(i, i ^ step) for i in range(devices)])  10.3 us
    all_to_all x1, blocking collectives, body(): mass = lax.all_to_all(mass, GROUP, 0, 0, tiled=True)  7.58 us
    all_to_all x1, blocking collectives, spread(): return lax.all_to_all(copies, axes, 0, 0, tiled=True)  7.4 us
    all_to_all x2, waiting for transfers between devices, spread(): return lax.all_to_all(copies, axes, 0, 0, tiled=True)  2.46 us
  transfers between devices with their start and end apart: 6, of which 5 were waited for; matrix products, arithmetic and copies ran while one was open for 0% of the time, Pallas kernels for 22%

profile of v9, /device:TPU:56, one launch (start us, length us, event | category | flops | bytes accessed | tf_op | source)
XLA Modules:
  0.0 120.5 jit_solution(6632545782129801004)
XLA Ops:
  0.0 0.8 copy-done
  0.8 0.8 broadcast_in_dim.6
  1.5 15.6 %all-to-all-start = ((bf16[16,64,128]{2,1,0:T(8,128)(2,1)}), bf16[16,64,128]{2,1,0:T(8,128)(2,1)S(1)}, u32[]{:S(2)}, u32[]{:S(2)}) async-start(bf16[16,64,128]{2,1,0:T(8,128)(2,1)} %broadcast_in_dim.6), calls=%async_computation | async-start | bytes 524288 | tf_op jit(solution)/shard_map/all_to_all | solution.py:201
  17.1 0.1 copy.4
  17.3 0.0 copy-start.1
  17.3 0.6 copy-done.1
  18.0 3.4 %collective-permute-start = (bf16[144,512]{1,0:T(8,128)(2,1)S(1)}, bf16[144,512]{1,0:T(8,128)(2,1)S(1)}, u32[]{:S(2)}, u32[]{:S(2)}) collective-permute-start(bf16[144,512]{1,0:T(8,128)(2,1)S(1)} %pad_maximum_fusion.refs_0_), channel_id=1, source_target_pairs={{0,1},{1,0},{64,65},{65,64},{2,3},{3,2},{66,67},{67,66},{4,5},{5,4... | collective-permute-start | bytes 442376 | tf_op jit(solution)/shard_map/ppermute | solution.py:218
  21.4 7.0 %collective-permute-done.refs_1_ = bf16[144,512]{1,0:T(8,128)(2,1)S(1)} collective-permute-done((bf16[144,512]{1,0:T(8,128)(2,1)S(1)}, bf16[144,512]{1,0:T(8,128)(2,1)S(1)}, u32[]{:S(2)}, u32[]{:S(2)}) %collective-permute-start) | collective-permute-done | bytes 147488 | tf_op jit(solution)/shard_map/ppermute | solution.py:218
  28.4 0.4 all-to-all-done
  28.7 1.2 %broadcast_in_dim.7 = bf16[4,16,64,128]{3,2,1,0:T(8,128)(2,1)} broadcast(bf16[16,64,128]{2,1,0:T(8,128)(2,1)S(1)} %all-to-all-done), dimensions={1,2,3} | broadcast | bytes 1310720 | tf_op jit(solution)/shard_map/broadcast_in_dim | solution.py:200
  30.0 4.3 %all-to-all-start.1 = ((bf16[4,16,64,128]{3,2,1,0:T(8,128)(2,1)}), bf16[4,16,64,128]{3,2,1,0:T(8,128)(2,1)S(1)}, u32[]{:S(2)}, u32[]{:S(2)}) async-start(bf16[4,16,64,128]{3,2,1,0:T(8,128)(2,1)} %broadcast_in_dim.7), calls=%async_computation.1 | async-start | bytes 2097152 | tf_op jit(solution)/shard_map/all_to_all | solution.py:201
  34.3 4.6 %collective-permute-start.1 = (bf16[144,512]{1,0:T(8,128)(2,1)S(1)}, bf16[144,512]{1,0:T(8,128)(2,1)S(1)}, u32[]{:S(2)}, u32[]{:S(2)}) collective-permute-start(bf16[144,512]{1,0:T(8,128)(2,1)S(1)} %pad_maximum_fusion.refs_0_), channel_id=1, source_target_pairs={{0,64},{1,65},{64,0},{65,1},{2,66},{3,67},{66,2},{67,3},{4,68},{5,... | collective-permute-start | bytes 442376 | tf_op jit(solution)/shard_map/ppermute | solution.py:218
  38.9 2.3 %collective-permute-start.2 = (bf16[144,512]{1,0:T(8,128)(2,1)S(1)}, bf16[144,512]{1,0:T(8,128)(2,1)S(1)}, u32[]{:S(2)}, u32[]{:S(2)}) collective-permute-start(bf16[144,512]{1,0:T(8,128)(2,1)S(1)} %pad_maximum_fusion.refs_0_), channel_id=1, source_target_pairs={{0,65},{1,64},{64,1},{65,0},{2,67},{3,66},{66,3},{67,2},{4,69},{5,... | collective-permute-start | bytes 442376 | tf_op jit(solution)/shard_map/ppermute | solution.py:218
  41.2 1.6 %collective-permute-done.1.refs_2_ = bf16[144,512]{1,0:T(8,128)(2,1)S(1)} collective-permute-done((bf16[144,512]{1,0:T(8,128)(2,1)S(1)}, bf16[144,512]{1,0:T(8,128)(2,1)S(1)}, u32[]{:S(2)}, u32[]{:S(2)}) %collective-permute-start.1) | collective-permute-done | bytes 147488 | tf_op jit(solution)/shard_map/ppermute | solution.py:218
  42.8 4.0 %collective-permute-done.2.refs_3_ = bf16[144,512]{1,0:T(8,128)(2,1)S(1)} collective-permute-done((bf16[144,512]{1,0:T(8,128)(2,1)S(1)}, bf16[144,512]{1,0:T(8,128)(2,1)S(1)}, u32[]{:S(2)}, u32[]{:S(2)}) %collective-permute-start.2) | collective-permute-done | bytes 147488 | tf_op jit(solution)/shard_map/ppermute | solution.py:218
  46.8 0.4 prepare.1
  47.2 2.1 %all-to-all-done.1.keys_ref = bf16[4,16,64,128]{3,2,1,0:T(8,128)(2,1)S(1)} async-done(((bf16[4,16,64,128]{3,2,1,0:T(8,128)(2,1)}), bf16[4,16,64,128]{3,2,1,0:T(8,128)(2,1)S(1)}, u32[]{:S(2)}, u32[]{:S(2)}) %all-to-all-start.1) | async-done | bytes 1048608 | tf_op jit(solution)/shard_map/all_to_all | solution.py:201
  49.3 1.9 %collective-permute-start.3 = (bf16[4,16,64,128]{3,2,1,0:T(8,128)(2,1)S(1)}, bf16[4,16,64,128]{3,2,1,0:T(8,128)(2,1)S(1)}, u32[]{:S(2)}, u32[]{:S(2)}) collective-permute-start(bf16[4,16,64,128]{3,2,1,0:T(8,128)(2,1)S(1)} %all-to-all-done.1.keys_ref), channel_id=1, source_target_pairs={{0,2},{2,0},{1,3},{3,1},{4,6},{6,4},{5,7},{7,5},{8,10},{10,8},{9,1... | collective-permute-start | bytes 3145736 | tf_op jit(solution)/shard_map/ppermute | solution.py:245
  51.2 26.6 %score.2 = (f32[64,2048]{1,0:T(8,128)S(1)}, f32[2,2048]{1,0:T(2,128)S(1)}) custom-call(f32[8,128]{1,0:T(8,128)S(1)} %get-tuple-element.20.most_ref, s32[4,128]{1,0:T(4,128)S(1)} %get-tuple-element.21.starts_ref, bf16[256,2048]{1,0:T(8,128)(2,1)S(1)} %get-tuple-element.24.lines_ref, bf16[4,16,64,128]{3,2,1,0:T(8,128)(2,1)S(1)} %all-to-all-done.1.keys_ref), custom_call_target="tpu_custom_call" | custom-call | flops 2147483648 | bytes 8388608 | tf_op jit(solution)/shard_map/score/pallas_call | solution.py:250
  77.9 26.7 %score.3 = (f32[64,2048]{1,0:T(8,128)S(1)}, f32[2,2048]{1,0:T(2,128)S(1)}, f32[2,2048]{1,0:T(2,128)S(1)}) custom-call(f32[8,128]{1,0:T(8,128)S(1)} %get-tuple-element.20.most_ref, s32[4,128]{1,0:T(4,128)S(1)} %get-tuple-element.21.starts_ref, bf16[256,2048]{1,0:T(8,128)(2,1)S(1)} %get-tuple-element.24.lines_ref, ...), custom_call_target="tpu_custom_call" | custom-call | flops 2147483648 | bytes 8388608 | tf_op jit(solution)/shard_map/score/pallas_call | solution.py:250
  104.6 7.4 %all_to_all.20.stat_ref = f32[4,2,2048]{2,1,0:T(2,128)S(1)} all-to-all(f32[4,2,2048]{2,1,0:T(2,128)S(1)} %broadcast_in_dim.8), channel_id=1, replica_groups=mesh['yh'=4,'yl'=2,'zh'=4,'x'=4,'core'=2,'head'=2] {'yl','head'}, dimensions={0} | all-to-all | bytes 131072 | tf_op jit(solution)/shard_map/all_to_all | solution.py:201
  112.0 0.1 mass.1
  112.1 7.6 %all_to_all.21.mass_ref = f32[4,2,2,16,128]{4,3,2,1,0:T(8,128)S(1)} all-to-all(f32[4,2,2,16,128]{4,3,2,1,0:T(8,128)S(1)} %bitcast.11), channel_id=1, replica_groups=mesh['yh'=4,'yl'=2,'zh'=4,'x'=4,'core'=2,'head'=2] {'yl','head'}, dimensions={0} | all-to-all | bytes 262144 | tf_op jit(solution)/shard_map/all_to_all | solution.py:283
  119.7 0.8 target.1
  (10 shorter events, 0.1 us)
Async XLA Ops:
  0.0 0.8 copy-start
  1.5 15.6 %copy-start.2 = (bf16[128,4,128]{2,1,0:T(4,128)(2,1)S(1)}, bf16[128,4,128]{2,1,0:T(4,128)(2,1)}, u32[]{:S(2)}) copy-start(bf16[128,4,128]{2,1,0:T(4,128)(2,1)} %param.3) | copy-start | bytes 393220
  1.5 27.2 %all-to-all-start = ((bf16[16,64,128]{2,1,0:T(8,128)(2,1)}), bf16[16,64,128]{2,1,0:T(8,128)(2,1)S(1)}, u32[]{:S(2)}, u32[]{:S(2)}) async-start(bf16[16,64,128]{2,1,0:T(8,128)(2,1)} %broadcast_in_dim.6), calls=%async_computation | async-start | bytes 524288 | tf_op jit(solution)/shard_map/all_to_all | solution.py:201
  17.3 0.7 copy-start.1
  18.0 10.4 %collective-permute-start = (bf16[144,512]{1,0:T(8,128)(2,1)S(1)}, bf16[144,512]{1,0:T(8,128)(2,1)S(1)}, u32[]{:S(2)}, u32[]{:S(2)}) collective-permute-start(bf16[144,512]{1,0:T(8,128)(2,1)S(1)} %pad_maximum_fusion.refs_0_), channel_id=1, source_target_pairs={{0,1},{1,0},{64,65},{65,64},{2,3},{3,2},{66,67},{67,66},{4,5},{5,4... | collective-permute-start | bytes 442376 | tf_op jit(solution)/shard_map/ppermute | solution.py:218
  30.0 19.3 %all-to-all-start.1 = ((bf16[4,16,64,128]{3,2,1,0:T(8,128)(2,1)}), bf16[4,16,64,128]{3,2,1,0:T(8,128)(2,1)S(1)}, u32[]{:S(2)}, u32[]{:S(2)}) async-start(bf16[4,16,64,128]{3,2,1,0:T(8,128)(2,1)} %broadcast_in_dim.7), calls=%async_computation.1 | async-start | bytes 2097152 | tf_op jit(solution)/shard_map/all_to_all | solution.py:201
  34.3 8.6 %collective-permute-start.1 = (bf16[144,512]{1,0:T(8,128)(2,1)S(1)}, bf16[144,512]{1,0:T(8,128)(2,1)S(1)}, u32[]{:S(2)}, u32[]{:S(2)}) collective-permute-start(bf16[144,512]{1,0:T(8,128)(2,1)S(1)} %pad_maximum_fusion.refs_0_), channel_id=1, source_target_pairs={{0,64},{1,65},{64,0},{65,1},{2,66},{3,67},{66,2},{67,3},{4,68},{5,... | collective-permute-start | bytes 442376 | tf_op jit(solution)/shard_map/ppermute | solution.py:218
  38.9 7.9 %collective-permute-start.2 = (bf16[144,512]{1,0:T(8,128)(2,1)S(1)}, bf16[144,512]{1,0:T(8,128)(2,1)S(1)}, u32[]{:S(2)}, u32[]{:S(2)}) collective-permute-start(bf16[144,512]{1,0:T(8,128)(2,1)S(1)} %pad_maximum_fusion.refs_0_), channel_id=1, source_target_pairs={{0,65},{1,64},{64,1},{65,0},{2,67},{3,66},{66,3},{67,2},{4,69},{5,... | collective-permute-start | bytes 442376 | tf_op jit(solution)/shard_map/ppermute | solution.py:218
  49.3 28.6 %collective-permute-start.3 = (bf16[4,16,64,128]{3,2,1,0:T(8,128)(2,1)S(1)}, bf16[4,16,64,128]{3,2,1,0:T(8,128)(2,1)S(1)}, u32[]{:S(2)}, u32[]{:S(2)}) collective-permute-start(bf16[4,16,64,128]{3,2,1,0:T(8,128)(2,1)S(1)} %all-to-all-done.1.keys_ref), channel_id=1, source_target_pairs={{0,2},{2,0},{1,3},{3,1},{4,6},{6,4},{5,7},{7,5},{8,10},{10,8},{9,1... | collective-permute-start | bytes 3145736 | tf_op jit(solution)/shard_map/ppermute | solution.py:245
